TPU v7x, 128 devices: a whole 4x4x4 slice. The times are simulated.
128 devices in a mesh: tm: 16 (over x, z), space: 8 (over y, core).
Axes of the slice: x: 4, y: 4, z: 4, core: 2. Of those that a mesh axis runs over, the one named last changes fastest.
Arguments:
- tokens: bfloat16 [131072, 2240], P(('tm', 'space')), may hold values from -256 to 256
- norm_gain: float32 [2240], replicated, may hold values from 0.1 to 1.9
- w_qkv: bfloat16 [2240, 3456], P(None, 'tm'), may hold values from -0.125 to 0.125
- w_out: bfloat16 [1152, 2240], P('tm'), may hold values from -0.1875 to 0.1875
- ffn_cached: bfloat16 [131072, 2240], P(('tm', 'space')), may hold values from -3 to 3
Outputs:
- mixed: bfloat16 [131072, 2240], P(('tm', 'space'))
All inputs are finite; a program needn't handle non-finite values.
Results may differ from a plain program's by a relative error of at most 0.0039.
Values may be sent and summed in bfloat16 or wider, within the bound.
No kernel may reach another device: no remote copies, remote signals or barrier semaphores. Data moves between devices by JAX's collectives and lax.ppermute only.
A program may use at most 128 MiB of HBM per device.

v0:
```python
import jax
import jax.numpy as jnp
from jax import lax
from jax.sharding import PartitionSpec as P

H = 36
HS = 32


def entering(part, axis, combine, identity):
    place = lax.axis_index(axis)
    gathered = jax.tree.map(lambda a: lax.all_gather(a, axis), part)
    state = jax.tree.map(lambda a, e: jnp.zeros_like(a) + jnp.asarray(e, a.dtype), part, identity)

    def one(lap, state):
        return combine(
            state, jax.tree.map(lambda a: lax.dynamic_index_in_dim(a, lap, 0, False), gathered)
        )

    return lax.fori_loop(0, place, one, state)


def add_pair(earlier, later):
    return (earlier[0] + later[0], earlier[1] + later[1])


def body(tokens, norm_gain, w_qkv, w_out, ffn_cached):
    inner = H * HS
    row_count = tokens.shape[0]
    floats = tokens.astype(jnp.float32)
    root_mean = jnp.sqrt(jnp.mean(floats * floats, axis=1, keepdims=True) + 1e-06)
    normed = (floats / root_mean * norm_gain).astype(jnp.bfloat16)
    projected = jnp.dot(
        normed, lax.all_gather(w_qkv, "tm", axis=1, tiled=True), preferred_element_type=jnp.float32
    )
    feat_q = jax.nn.relu(projected[:, :inner]).astype(jnp.bfloat16)
    feat_k = jax.nn.relu(projected[:, inner : 2 * inner]).astype(jnp.bfloat16)
    values = projected[:, 2 * inner :].astype(jnp.bfloat16)
    kv_state = jnp.einsum(
        "thi,thj->ihj",
        feat_k.reshape(row_count, H, HS),
        values.reshape(row_count, H, HS),
        preferred_element_type=jnp.float32,
    ).reshape(HS, inner)
    key_sum = jnp.sum(feat_k, axis=0, keepdims=True, dtype=jnp.float32)
    empty_pair = (jnp.zeros_like(kv_state), jnp.zeros_like(key_sum))
    slab_total = lax.psum((kv_state, key_sum), "space")
    before = entering(slab_total, "tm", add_pair, empty_pair)
    seen_state, seen_norm = add_pair(before, slab_total)
    queries = feat_q.reshape(row_count, H, HS)
    numerator = jnp.einsum(
        "thi,ihj->thj",
        queries,
        seen_state.reshape(HS, H, HS),
        precision=lax.Precision.HIGHEST,
        preferred_element_type=jnp.float32,
    )
    denominator = (
        jnp.einsum(
            "thi,hi->th",
            queries,
            seen_norm.reshape(H, HS),
            precision=lax.Precision.HIGHEST,
            preferred_element_type=jnp.float32,
        )
        + 1e-06
    )
    attended = (numerator / denominator[:, :, None]).reshape(row_count, inner).astype(jnp.bfloat16)
    branch_out = jnp.dot(
        attended,
        lax.all_gather(w_out, "tm", axis=0, tiled=True),
        preferred_element_type=jnp.float32,
    )
    return (branch_out + ffn_cached.astype(jnp.float32)).astype(jnp.bfloat16)


def solution(mesh):
    return jax.shard_map(
        body,
        mesh=mesh,
        in_specs=(
            P(("tm", "space"), None),
            P(),
            P(None, "tm"),
            P("tm", None),
            P(("tm", "space"), None),
        ),
        out_specs=P(("tm", "space"), None),
        check_vma=False,
    )
```

profile of v0, /device:TPU:1, one launch (start us, length us, event | category | flops | bytes accessed | tf_op | source)
XLA Modules:
  0.0 339.4 jit_solution(692750318596810389)
XLA Ops:
  6.5 0.0 copy-start.1
  6.5 0.0 all-gather.7.cloned.1.call-start
  6.5 0.7 all-gather.7.cloned.1.call-update
  7.3 0.0 all-reduce.2.cloned.1.call-start
  7.3 3.3 fusion
  10.6 109.3 %all-gather.7.cloned.1.call-done = bf16[2240,3456]{0,1:T(8,128)(2,1)} async-done(((bf16[2240,216]{0,1:T(8,128)(2,1)}), bf16[2240,3456]{0,1:T(8,128)(2,1)}) %all-gather.7.cloned.1.call-update) | async-done | bytes 15482896 | tf_op jit(solution)/shard_map/all_gather | solution.py:34
  119.9 0.0 copy-done.1
  119.9 24.4 %fusion.6 = bf16[1024,3456]{1,0:T(8,128)(2,1)S(1)} fusion(bf16[2240,3456]{0,1:T(8,128)(2,1)} %all-gather.7.cloned.1.call-done, bf16[1024,2240]{0,1:T(8,128)(2,1)} %param.7, f32[2240]{0:T(1024)S(1)} %copy-done.1, f32[1024]{0:T(1024)S(1)} %add_sqrt_fusion), kind=kOutput, calls=%fused_computation.16 | convolution fusion | flops 15863644160 | bytes 27161344 | tf_op jit(solution)/shard_map/dot_general | solution.py:33
  144.3 2.8 fusion.3
  147.0 0.7 convert_reduce_fusion
  147.7 4.3 %copy.16 = bf16[1024,1152]{0,1:T(8,128)(2,1)} copy(bf16[1024,1152]{1,0:T(8,128)(2,1)} %get-tuple-element.56) | data formatting | bytes 4718592 | tf_op jit(solution)/shard_map/slice | solution.py:38
  152.0 2.5 copy.17
  154.5 3.1 fusion.12
  157.6 0.9 copy.18
  158.5 0.0 all-reduce.2.cloned.1.call-update
  158.5 0.0 all-gather.11.cloned.1.call-start
  158.6 55.6 %all-reduce.2.cloned.1.call-done = f32[32,1152]{1,0:T(8,128)} async-done(((f32[32,1152]{1,0:T(8,128)}), f32[32,1152]{1,0:T(8,128)}) %all-reduce.2.cloned.1.call-update) | async-done | bytes 147472 | tf_op jit(solution)/shard_map/psum | solution.py:47
  214.1 0.0 copy-start
  214.1 0.0 all-gather.11.cloned.1.call-update
  214.2 0.0 all-gather.9.cloned.1.call-start
  214.2 0.5 all-gather.9.cloned.1.call-update
  214.8 2.8 copy.19
  217.6 14.5 %psum.15 = f32[1,1152]{1,0:T(1,128)S(1)} all-reduce(f32[1,1152]{1,0:T(1,128)S(1)} %broadcast_in_dim.14), channel_id=1, replica_groups=mesh['tm'=16,'space'=8] {'space'}, use_global_device_ids=true, to_apply=%region_3.4 | all-reduce | flops 1152 | bytes 9216 | tf_op jit(solution)/shard_map/psum | solution.py:47
  232.1 18.8 %all-gather.2 = f32[16,1,1152]{2,1,0:T(1,128)S(1)} all-gather(f32[1,1,1152]{2,1,0:T(1,128)S(1)} %bitcast.44), channel_id=3, replica_groups=mesh['tm'=16,'space'=8] {'tm'}, dimensions={0}, use_global_device_ids=true | all-gather | bytes 78336 | tf_op jit(solution)/shard_map/all_gather | solution.py:12
  250.9 11.4 %all-gather.11.cloned.1.call-done = f32[512,1152]{1,0:T(8,128)} async-done(((f32[32,1152]{1,0:T(8,128)}), f32[512,1152]{1,0:T(8,128)}) %all-gather.11.cloned.1.call-update) | async-done | bytes 2359312 | tf_op jit(solution)/shard_map/all_gather | solution.py:12
  262.4 0.2 while.12
  262.6 0.1 reshape.44
  262.7 0.0 copy-done
  262.7 0.2 copy.23
  263.0 1.0 fusion.13
  264.1 3.6 %fusion.5 = bf16[1024,36,32]{0,2,1:T(8,128)(2,1)} fusion(f32[1024,36]{0,1:T(8,128)S(1)} %fusion.10, f32[32,36,32]{0,2,1:T(8,128)S(1)} %bitcast.42, bf16[1024,36,32]{0,2,1:T(8,128)(2,1)S(1)} %bitcast.38), kind=kOutput, calls=%fused_computation.14 | convolution fusion | flops 455344128 | bytes 5013504 | tf_op jit(solution)/shard_map/thi,ihj->thj/dot_general | solution.py:51
  267.6 53.9 %all-gather.9.cloned.1.call-done = bf16[1152,2240]{1,0:T(8,128)(2,1)} async-done(((bf16[72,2240]{1,0:T(8,128)(2,1)}), bf16[1152,2240]{1,0:T(8,128)(2,1)}) %all-gather.9.cloned.1.call-update) | async-done | bytes 5160976 | tf_op jit(solution)/shard_map/all_gather | solution.py:71
  321.5 11.3 %add_convert_fusion = bf16[1024,2240]{0,1:T(8,128)(2,1)} fusion(bf16[1024,2240]{0,1:T(8,128)(2,1)} %param.11, bf16[1024,1152]{0,1:T(8,128)(2,1)} %bitcast.45, bf16[1152,2240]{1,0:T(8,128)(2,1)} %all-gather.9.cloned.1.call-done), kind=kOutput, calls=%fused_computation.7 | convolution fusion | flops 5291704320 | bytes 16695296 | tf_op jit(solution)/shard_map/dot_general | solution.py:69
  (7 shorter events, 0.1 us)
Async XLA Ops:
  6.5 113.4 %copy-start.1 = (f32[2240]{0:T(1024)S(1)}, f32[2240]{0:T(1024)}, u32[]{:S(2)}) copy-start(f32[2240]{0:T(1024)} %param.8) | copy-start | bytes 26884
  6.5 113.3 %all-gather.7.cloned.1.call-start = ((), (), s32[]{:S(2)}) async-start(), calls=%async_computation | async-start | bytes 16920576 | tf_op jit(solution)/shard_map/all_gather | solution.py:34
  7.3 206.9 %all-reduce.2.cloned.1.call-start = ((), (), s32[]{:S(2)}) async-start(), calls=%async_computation.1 | async-start | bytes 294912 | tf_op jit(solution)/shard_map/psum | solution.py:47
  158.5 103.8 %all-gather.11.cloned.1.call-start = ((), (), s32[]{:S(2)}) async-start(), calls=%async_computation.3 | async-start | bytes 2506752 | tf_op jit(solution)/shard_map/all_gather | solution.py:12
  214.1 48.6 %copy-start = (f32[32,1152]{1,0:T(8,128)S(1)}, f32[32,1152]{1,0:T(8,128)}, u32[]{:S(2)}) copy-start(f32[32,1152]{1,0:T(8,128)} %all-reduce.2.cloned.1.call-done) | copy-start | bytes 442372
  214.2 107.3 %all-gather.9.cloned.1.call-start = ((), (), s32[]{:S(2)}) async-start(), calls=%async_computation.2 | async-start | bytes 5640192 | tf_op jit(solution)/shard_map/all_gather | solution.py:71
Sparse Core Ops, SparseCore 0:
  9.6 110.2 all-gather.6
  158.6 55.4 all-reduce.1
  216.6 45.7 all-gather.10
  264.6 56.7 all-gather.8
where the time goes:
time: 340 us; the launch traced here: 339 us
  waiting for transfers between devices  231 us (68%)
  matrix products  43.4 us (13%)
  blocking collectives  33.3 us (10%)
  between operations  13.2 us (4%)
  local copies, waits for them, and re-layouts  10.8 us (3%)
  other arithmetic  6.82 us (2%)
    all_gather x1, waiting for transfers between devices, body(): lax.all_gather(w_qkv, 'tm', axis=1, tiled=True)  109 us
    psum x1, waiting for transfers between devices, body(): slab_total = lax.psum((kv_state, key_sum), 'space')  55.6 us
    all_gather x1, waiting for transfers between devices, body(): lax.all_gather(w_out, 'tm', axis=0, tiled=True)  53.9 us
    dot_general x1, matrix products, body(): jnp.dot(normed, lax.all_gather(w_qkv, 'tm', axis=1, tiled=True), preferre...  24.4 us
    all_gather x1, blocking collectives, entering(): gathered = jax.tree.map(lambda a: lax.all_gather(a, axis), part)  18.8 us
    psum x1, blocking collectives, body(): slab_total = lax.psum((kv_state, key_sum), 'space')  14.5 us
    all_gather x1, waiting for transfers between devices, entering(): gathered = jax.tree.map(lambda a: lax.all_gather(a, axis), part)  11.4 us
    dot_general x1, matrix products, body(): jnp.dot(attended, lax.all_gather(w_out, 'tm', axis=0, tiled=True), prefer...  11.3 us
  transfers between devices with their start and end apart: 4, of which 4 were waited for; matrix products, arithmetic and copies ran while one was open for 3% of the time, Pallas kernels for 0%

commit v1 on v0

v1 whole, which is shorter than its diff:
```python
import jax
import jax.numpy as jnp
import numpy as np
from jax import lax
from jax.experimental import pallas as pl
from jax.experimental.pallas import tpu as pltpu
from jax.sharding import PartitionSpec as P

H = 36
HS = 32
INNER = H * HS
GROUPS = INNER // 128
THIRD = 72
BOTH = ("tm", "space")
F32 = jnp.float32
BF16 = jnp.bfloat16

FIRST = {2: 6, 3: 7, 4: 8, 1: 9, 0: 10}
SECOND = {0: 12, 1: 13, 2: 14, 3: 15, 4: 11}


def device(t, y, c):
    return t * 8 + y * 2 + c


def trade_pairs():
    pairs = []
    for y in range(4):
        for d in range(5):
            a, b = FIRST[d], SECOND[d]
            pairs += [
                (device(d, y, 0), device(a, y, 0)),
                (device(a, y, 0), device(d, y, 0)),
                (device(d, y, 1), device(b, y, 0)),
                (device(b, y, 1), device(d, y, 1)),
            ]
    return pairs


def kv_third(t, c):
    if t <= 4:
        return 3 * (FIRST, SECOND)[c][t]
    return 3 * t + 1 + c


def q_third(t):
    if t <= 5:
        return 3 * t
    for d in range(5):
        if FIRST[d] == t:
            return 3 * d + 1
        if SECOND[d] == t:
            return 3 * d + 2


def along(core_axes):
    groups = {}
    for t in range(16):
        x, z = divmod(t, 4)
        for y in range(4):
            for c in range(2):
                fixed = z if core_axes[c] == "x" else x
                groups.setdefault((y, c, fixed), []).append(device(t, y, c))
    return list(groups.values())


def gather(part):
    part = lax.all_gather(part, BOTH, axis=0, tiled=True, axis_index_groups=along("zx"))
    return lax.all_gather(part, BOTH, axis=0, tiled=True, axis_index_groups=along("xz"))


def other_core(a):
    return lax.ppermute(a, "space", [(i, i ^ 1) for i in range(8)])


def state_kernel(k_ref, v_ref, out_ref):
    keys = jnp.maximum(k_ref[...], 0)
    contract = (((1,), (1,)), ((), ()))
    full = lax.dot_general(keys, v_ref[...], contract, preferred_element_type=F32)
    head = lax.broadcasted_iota(jnp.int32, (HS, 128), 1) // HS
    state = full[:HS]
    for b in range(1, 4):
        state = jnp.where(head == b, full[b * HS : (b + 1) * HS], state)
    out_ref[0, :HS, :] = state
    out_ref[0, HS:, :] = lax.dot_general(
        jnp.ones((8, keys.shape[1]), BF16), keys, contract, preferred_element_type=F32
    )


def block_states(keys, values):
    rows = keys.shape[1]
    spec = pl.BlockSpec((128, rows), lambda g: (g, 0))
    return pl.pallas_call(
        state_kernel,
        grid=(GROUPS,),
        in_specs=[spec, spec],
        out_specs=pl.BlockSpec((1, HS + 8, 128), lambda g: (g, 0, 0)),
        out_shape=jax.ShapeDtypeStruct((GROUPS, HS + 8, 128), F32),
        compiler_params=pltpu.CompilerParams(vmem_limit_bytes=32 * 2**20),
        cost_estimate=pl.CostEstimate(flops=2 * 128 * INNER * rows, bytes_accessed=4 * INNER * rows, transcendentals=0),
    )(keys, values)


def split_dot(a, b):
    total = None
    for _ in range(3):
        high = a.astype(BF16)
        part = jnp.dot(high, b, preferred_element_type=F32)
        total = part if total is None else total + part
        a = a - high.astype(F32)
    return total


def attend_kernel(q_ref, seen_ref, out_ref):
    queries = jnp.maximum(q_ref[...], 0)
    row = lax.broadcasted_iota(jnp.int32, (128, 128), 0) // HS
    column = lax.broadcasted_iota(jnp.int32, (128, 128), 1) // HS
    same = row == column
    state = jnp.where(same, jnp.concatenate([seen_ref[0, :HS, :]] * 4, axis=0), 0.0)
    norm = jnp.where(same, jnp.broadcast_to(seen_ref[0, HS : HS + 1, :], (128, 128)), 0.0)
    numerator = split_dot(state.T, queries)
    denominator = split_dot(norm, queries) + 1e-06
    out_ref[...] = (numerator / denominator).astype(BF16)


def attend(queries, seen):
    rows = queries.shape[1]
    return pl.pallas_call(
        attend_kernel,
        grid=(GROUPS,),
        in_specs=[
            pl.BlockSpec((128, rows), lambda g: (g, 0)),
            pl.BlockSpec((1, HS + 8, 128), lambda g: (g, 0, 0)),
        ],
        out_specs=pl.BlockSpec((128, rows), lambda g: (g, 0)),
        out_shape=jax.ShapeDtypeStruct((INNER, rows), BF16),
        compiler_params=pltpu.CompilerParams(vmem_limit_bytes=32 * 2**20),
        cost_estimate=pl.CostEstimate(flops=12 * 128 * INNER * rows, bytes_accessed=4 * INNER * rows, transcendentals=0),
    )(queries, seen)


def sync(state, core):
    keep = lax.dynamic_slice_in_dim(state, 4 * core, 5, 0)
    give = lax.dynamic_slice_in_dim(state, 4 * (1 - core), 5, 0)
    keep = keep + other_core(give)
    for bit in (2, 4):
        keep = keep + lax.ppermute(keep, "space", [(i, i ^ bit) for i in range(8)])
    for step in (1, 2, 4, 8):
        keep = keep + lax.ppermute(keep, "tm", [(t, t + step) for t in range(16 - step)])
    theirs = other_core(keep)
    low = jnp.where(core == 0, keep, theirs)
    high = jnp.where(core == 0, theirs, keep)
    return jnp.concatenate([low, high[1:]], axis=0)


def body(tokens, norm_gain, w_qkv, w_out, ffn_cached):
    t = lax.axis_index("tm")
    core = lax.rem(lax.axis_index("space"), 2)
    rows = tokens.shape[0]
    weights = w_qkv.T
    local = lambda j: lax.dynamic_slice_in_dim(weights, THIRD * j, THIRD, 0)

    given = local(jnp.where(t <= 4, 1 + core, 0))
    traded = lax.ppermute(given, BOTH, trade_pairs())
    part_kv = jnp.where(t <= 4, traded, local(1 + core))
    part_qo = jnp.where(core == 0, jnp.where(t >= 6, traded, weights[:THIRD]), w_out)

    floats = tokens.T.astype(F32)
    root_mean = jnp.sqrt(jnp.mean(floats * floats, axis=0, keepdims=True) + 1e-06)
    normed = (floats / root_mean * norm_gain[:, None]).astype(BF16)

    mine_kv = gather(part_kv)
    theirs_kv = other_core(mine_kv)
    project = lambda w: jnp.dot(w, normed, preferred_element_type=F32).astype(BF16)
    mine, theirs = project(mine_kv), project(theirs_kv)
    slots = (
        jnp.where(core == 0, mine, theirs).reshape(4, 4, THIRD, rows),
        jnp.where(core == 0, theirs, mine).reshape(4, 4, THIRD, rows),
    )
    thirds = {}
    for s in range(16):
        x, z = divmod(s, 4)
        thirds[kv_third(s, 0)] = slots[0][x, z]
        thirds[kv_third(s, 1)] = slots[1][z, x]
    keys = jnp.concatenate([thirds[u] for u in range(16, 32)], axis=0)
    values = jnp.concatenate([thirds[u] for u in range(32, 48)], axis=0)
    state = block_states(keys, values)

    part_qo, _ = lax.optimization_barrier((part_qo, mine_kv))
    mine_qo = gather(part_qo)
    theirs_qo = other_core(mine_qo)
    w_q = jnp.where(core == 0, mine_qo, theirs_qo)
    w_o = jnp.where(core == 0, theirs_qo, mine_qo).reshape(4, 4, THIRD, -1)
    w_o = w_o.transpose(1, 0, 2, 3).reshape(INNER, -1)
    projected = project(w_q).reshape(16, THIRD, rows)
    order = {q_third(s): s for s in range(16)}
    queries = jnp.concatenate([projected[order[u]] for u in range(16)], axis=0)

    seen = sync(state, core)
    attended = attend(queries, seen)
    branch_out = lax.dot_general(w_o, attended, (((0,), (0,)), ((), ())), preferred_element_type=F32)
    return (branch_out + ffn_cached.T.astype(F32)).astype(BF16).T


def solution(mesh):
    return jax.shard_map(
        body,
        mesh=mesh,
        in_specs=(
            P(("tm", "space"), None),
            P(),
            P(None, "tm"),
            P("tm", None),
            P(("tm", "space"), None),
        ),
        out_specs=P(("tm", "space"), None),
        check_vma=False,
    )
```

time: 340 us -> 291 us (0.86)
  waiting for transfers between devices: 231 us -> 122 us
  local copies, waits for them, and re-layouts: 10.8 us -> 55.2 us
  starting transfers between devices: 0.12 us -> 37.6 us
  blocking collectives: 33.3 us -> 0 us
  Pallas kernels: 0 us -> 12 us
  matrix products: 43.4 us -> 37.2 us
  other arithmetic: 6.82 us -> 11.3 us
    all_gather x3 -> x4, waiting for transfers between devices: 175 us -> 103 us  [the longest x2 52 us: gather(): lax.all_gather(part, BOTH, axis=0, tiled=True, axis_index_groups=along('x...]
    psum x1 -> x0, waiting for transfers between devices: 55.6 us -> none  [body(): slab_total = lax.psum((kv_state, key_sum), 'space')]
    ppermute x0 -> x11, starting transfers between devices: none -> 37.5 us  [the longest x4 19.4 us: sync(): lax.ppermute(keep, 'tm', [(t, t + step) for t in range(16 - step)])]
    unnamed x4 -> x49, local copies, waits for them, and re-layouts: 0.01 us -> 23.2 us
    all_gather x1 -> x0, blocking collectives: 18.8 us -> none  [entering(): gathered = jax.tree.map(lambda a: lax.all_gather(a, axis), part)]
    ppermute x0 -> x11, waiting for transfers between devices: none -> 18.3 us  [the longest x4 6.62 us: sync(): lax.ppermute(keep, 'tm', [(t, t + step) for t in range(16 - step)])]
    all_gather x0 -> x2, local copies, waits for them, and re-layouts: none -> 17 us  [gather(): lax.all_gather(part, BOTH, axis=0, tiled=True, axis_index_groups=along('x...]
    psum x1 -> x0, blocking collectives: 14.5 us -> none  [body(): slab_total = lax.psum((kv_state, key_sum), 'space')]
  transfers between devices with their start and end apart: 4 -> 15, of which waited for: 4 -> 13; matrix products, arithmetic and copies ran while one was open for 3% -> 16% of each run, Pallas kernels for 0% -> 2%
where the time goes in v1:
time: 291 us; the launch traced here: 289 us
  waiting for transfers between devices  122 us (42%)
  local copies, waits for them, and re-layouts  55.2 us (19%)
  starting transfers between devices  37.6 us (13%)
  matrix products  37.2 us (13%)
  between operations  13.5 us (5%)
  Pallas kernels  12 us (4%)
  other arithmetic  11.3 us (4%)
    all_gather x2, waiting for transfers between devices, gather(): lax.all_gather(part, BOTH, axis=0, tiled=True, axis_index_groups=along('x...  52 us
    all_gather x2, waiting for transfers between devices, gather(): lax.all_gather(part, BOTH, axis=0, tiled=True, axis_index_groups=along('z...  51.4 us
    dot_general x3, matrix products, body(): jnp.dot(w, normed, preferred_element_type=F32).astype(BF16)  27.8 us
    unnamed x49, local copies, waits for them, and re-layouts  23.2 us
    ppermute x4, starting transfers between devices, sync(): lax.ppermute(keep, 'tm', [(t, t + step) for t in range(16 - step)])  19.4 us
    all_gather x2, local copies, waits for them, and re-layouts, gather(): lax.all_gather(part, BOTH, axis=0, tiled=True, axis_index_groups=along('x...  17 us
    dot_general x1, matrix products, body(): lax.dot_general(w_o, attended, (((0,), (0,)), ((), ())), preferred_elemen...  9.43 us
    ppermute x1, local copies, waits for them, and re-layouts, other_core(): return lax.ppermute(a, 'space', [(i, i ^ 1) for i in range(8)])  8.53 us
  transfers between devices with their start and end apart: 15, of which 13 were waited for; matrix products, arithmetic and copies ran while one was open for 16% of the time, Pallas kernels for 2%

profile of v1, /device:TPU:1, one launch (start us, length us, event | category | flops | bytes accessed | tf_op | source)
XLA Modules:
  0.0 288.6 jit_solution(10475350441046897828)
XLA Ops:
  6.5 1.0 dynamic-slice_bitcast_fusion
  7.5 5.8 %collective-permute-start = (bf16[72,2240]{1,0:T(8,128)(2,1)S(1)}, bf16[72,2240]{1,0:T(8,128)(2,1)S(1)}, u32[]{:S(2)}, u32[]{:S(2)}) collective-permute-start(bf16[72,2240]{1,0:T(8,128)(2,1)S(1)} %dynamic-slice_bitcast_fusion), channel_id=1, source_target_pairs={{0,80},{80,0},{1,96},{97,1},{8,72},{72,8},{9,104},{105,9},{16,48},... | collective-permute-start | bytes 967688 | tf_op jit(solution)/shard_map/ppermute | solution.py:164
  13.3 4.0 %collective-permute-done = bf16[72,2240]{1,0:T(8,128)(2,1)S(1)} collective-permute-done((bf16[72,2240]{1,0:T(8,128)(2,1)S(1)}, bf16[72,2240]{1,0:T(8,128)(2,1)S(1)}, u32[]{:S(2)}, u32[]{:S(2)}) %collective-permute-start) | collective-permute-done | bytes 322592 | tf_op jit(solution)/shard_map/ppermute | solution.py:164
  17.4 2.2 bitcast_select_fusion
  19.6 0.0 all-gather.7.cloned.1.call-start
  19.6 29.7 %all-gather.5.cloned.1.call-done = bf16[288,2240]{1,0:T(8,128)(2,1)} async-done(((bf16[72,2240]{1,0:T(8,128)(2,1)}), bf16[288,2240]{1,0:T(8,128)(2,1)}) %all-gather.5.cloned.1.call-update) | async-done | bytes 1290256 | tf_op jit(solution)/shard_map/all_gather | solution.py:68
  49.4 40.4 %all-gather.7.cloned.1.call-done = bf16[1152,2240]{1,0:T(8,128)(2,1)} async-done(((bf16[288,2240]{1,0:T(8,128)(2,1)}), bf16[1152,2240]{1,0:T(8,128)(2,1)}) %all-gather.7.cloned.1.call-update) | async-done | bytes 5160976 | tf_op jit(solution)/shard_map/all_gather | solution.py:69
  89.8 8.5 %copy.14 = bf16[1152,2240]{0,1:T(8,128)(2,1)} copy(bf16[1152,2240]{1,0:T(8,128)(2,1)} %all-gather.7.cloned.1.call-done) | data formatting | bytes 10321920 | tf_op jit(solution)/shard_map/all_gather | solution.py:69
  98.3 0.6 collective-permute-start.2
  98.9 0.0 all-gather.11.cloned.1.call-start
  99.0 21.7 %all-gather.9.cloned.1.call-done = bf16[288,2240]{1,0:T(8,128)(2,1)} async-done(((bf16[72,2240]{1,0:T(8,128)(2,1)}), bf16[288,2240]{1,0:T(8,128)(2,1)}) %all-gather.9.cloned.1.call-update) | async-done | bytes 1290256 | tf_op jit(solution)/shard_map/all_gather | solution.py:68
  120.7 3.5 %fusion = f32[1024]{0:T(1024)S(1)} fusion(bf16[1024,2240]{0,1:T(8,128)(2,1)} %param.5), kind=kLoop, calls=%fused_computation.2 | loop fusion | flops 6880256 | bytes 4591616 | tf_op jit(solution)/shard_map/reduce_sum | solution.py:169
  124.2 9.3 %convolution_convert_fusion.1 = bf16[1152,1024]{1,0:T(8,128)(2,1)S(1)} fusion(bf16[1152,2240]{1,0:T(8,128)(2,1)} %all-gather.7.cloned.1.call-done, bf16[1024,2240]{0,1:T(8,128)(2,1)} %param.5, f32[2240]{0:T(1024)S(1)} %copy-done.3, f32[1024]{0:T(1024)S(1)} %add_sqrt_fusion), kind=kOutput, calls=%fused_computation.11 | convolution fusion | flops 5295177728 | bytes 12120832 | tf_op jit(solution)/shard_map/dot_general | solution.py:174
  133.5 9.1 %broadcast_select_fusion.1 = (bf16[1152,1024]{1,0:T(8,128)(2,1)S(1)}, bf16[1152,1024]{1,0:T(8,128)(2,1)S(1)}) fusion(bf16[1152,1024]{1,0:T(8,128)(2,1)S(1)} %convolution_convert_fusion.1, pred[]{:T(512)S(6)} %eq.2, bf16[1152,2240]{0,1:T(8,128)(2,1)} %collective-permute-done.2, bf16[1024,2240]{0,1:T(8,128)(2,1)S(1)} %bitcast.146, f32[2240]{0:T(1024)S(1)} %copy-done.3, ...), kind=kOutput, calls=%fused_computation.13 | convolution fusion | flops 5297537024 | bytes 16839424 | tf_op jit(solution)/shard_map/dot_general | solution.py:174
  142.7 0.7 fusion.25
  143.4 1.1 fusion.24
  144.5 0.7 fusion.23
  145.2 0.7 fusion.22
  145.9 0.7 fusion.21
  146.6 0.7 fusion.20
  147.2 0.7 fusion.19
  147.9 0.7 fusion.18
  148.6 0.7 fusion.17
  149.3 11.7 %all-gather.11.cloned.1.call-done = bf16[1152,2240]{1,0:T(8,128)(2,1)} async-done(((bf16[288,2240]{1,0:T(8,128)(2,1)}), bf16[1152,2240]{1,0:T(8,128)(2,1)}) %all-gather.11.cloned.1.call-update) | async-done | bytes 5160976 | tf_op jit(solution)/shard_map/all_gather | solution.py:69
  161.0 8.5 %copy.12 = bf16[1152,2240]{0,1:T(8,128)(2,1)} copy(bf16[1152,2240]{1,0:T(8,128)(2,1)} %all-gather.11.cloned.1.call-done) | data formatting | bytes 10321920 | tf_op jit(solution)/shard_map/all_gather | solution.py:69
  169.5 0.6 collective-permute-start.1
  170.1 1.7 fusion.16
  171.7 0.9 fusion.39
  172.7 0.9 fusion.38
  173.6 1.7 fusion.15
  175.3 0.9 fusion.36
  176.2 1.7 fusion.14
  177.8 1.7 fusion.13
  179.5 0.9 fusion.33
  180.4 0.9 fusion.32
  181.4 1.7 fusion.12
  183.0 0.9 fusion.30
  183.9 1.7 fusion.11
  185.6 1.7 fusion.10
  187.3 0.9 fusion.27
  188.2 0.9 fusion.26.k_ref
  189.1 6.2 %shard_map.55 = f32[9,40,128]{2,1,0:T(8,128)S(1)} custom-call(bf16[1152,1024]{1,0:T(8,128)(2,1)S(1)} %fusion.26.k_ref, bf16[1152,1024]{1,0:T(8,128)(2,1)} %get-tuple-element.9.v_ref), custom_call_target="tpu_custom_call" | custom-call | flops 301989888 | bytes 4718592 | tf_op jit(solution)/shard_map/pallas_call | solution.py:93
  195.4 0.1 collective-permute-start.3
  195.5 1.3 collective-permute-done.3
  196.8 1.3 collective-permute-start.4
  198.1 3.1 %collective-permute-done.4 = f32[5,40,128]{2,1,0:T(8,128)S(1)} collective-permute-done((f32[5,40,128]{2,1,0:T(8,128)S(1)}, f32[5,40,128]{2,1,0:T(8,128)S(1)}, u32[]{:S(2)}, u32[]{:S(2)}) %collective-permute-start.4) | collective-permute-done | bytes 102432 | tf_op jit(solution)/shard_map/ppermute | solution.py:147
  201.2 2.8 collective-permute-start.5
  204.0 2.3 collective-permute-done.5
  206.3 3.2 %collective-permute-start.6 = (f32[5,40,128]{2,1,0:T(8,128)S(1)}, f32[5,40,128]{2,1,0:T(8,128)S(1)}, u32[]{:S(2)}, u32[]{:S(2)}) collective-permute-start(f32[5,40,128]{2,1,0:T(8,128)S(1)} %add.61), channel_id=1, source_target_pairs={{0,8},{8,16},{16,24},{24,32},{32,40},{40,48},{48,56},{56,64},{64,7... | collective-permute-start | bytes 307208 | tf_op jit(solution)/shard_map/ppermute | solution.py:149
  209.5 1.7 collective-permute-done.6
  211.2 5.3 %collective-permute-start.7 = (f32[5,40,128]{2,1,0:T(8,128)S(1)}, f32[5,40,128]{2,1,0:T(8,128)S(1)}, u32[]{:S(2)}, u32[]{:S(2)}) collective-permute-start(f32[5,40,128]{2,1,0:T(8,128)S(1)} %add.62), channel_id=1, source_target_pairs={{0,16},{8,24},{16,32},{24,40},{32,48},{40,56},{48,64},{56,72},{64,... | collective-permute-start | bytes 307208 | tf_op jit(solution)/shard_map/ppermute | solution.py:149
  216.5 1.7 collective-permute-done.7
  218.2 6.1 %collective-permute-start.8 = (f32[5,40,128]{2,1,0:T(8,128)S(1)}, f32[5,40,128]{2,1,0:T(8,128)S(1)}, u32[]{:S(2)}, u32[]{:S(2)}) collective-permute-start(f32[5,40,128]{2,1,0:T(8,128)S(1)} %add.63), channel_id=1, source_target_pairs={{0,32},{8,40},{16,48},{24,56},{32,64},{40,72},{48,80},{56,88},{64,... | collective-permute-start | bytes 307208 | tf_op jit(solution)/shard_map/ppermute | solution.py:149
  224.3 1.7 collective-permute-done.8
  226.0 4.7 %collective-permute-start.9 = (f32[5,40,128]{2,1,0:T(8,128)S(1)}, f32[5,40,128]{2,1,0:T(8,128)S(1)}, u32[]{:S(2)}, u32[]{:S(2)}) collective-permute-start(f32[5,40,128]{2,1,0:T(8,128)S(1)} %add.64), channel_id=1, source_target_pairs={{0,64},{8,72},{16,80},{24,88},{32,96},{40,104},{48,112},{56,120},{... | collective-permute-start | bytes 307208 | tf_op jit(solution)/shard_map/ppermute | solution.py:149
  230.8 1.7 collective-permute-done.9
  232.4 6.9 %collective-permute-start.10 = (f32[5,40,128]{2,1,0:T(8,128)S(1)}, f32[5,40,128]{2,1,0:T(8,128)S(1)}, u32[]{:S(2)}, u32[]{:S(2)}) collective-permute-start(f32[5,40,128]{2,1,0:T(8,128)S(1)} %add.65), channel_id=1, source_target_pairs={{0,1},{1,0},{2,3},{3,2},{4,5},{5,4},{6,7},{7,6},{8,9},{9,8},{10,11... | collective-permute-start | bytes 307208 | tf_op jit(solution)/shard_map/ppermute | solution.py:73
  239.3 0.9 collective-permute-done.10
  240.3 8.5 %copy.13 = bf16[1152,2240]{1,0:T(8,128)(2,1)} copy(bf16[1152,2240]{0,1:T(8,128)(2,1)} %collective-permute-done.1) | data formatting | bytes 10321920 | tf_op jit(solution)/shard_map/ppermute | solution.py:73
  248.9 9.4 %fusion.6 = bf16[1152,1024]{1,0:T(8,128)(2,1)S(1)} fusion(bf16[1152,2240]{1,0:T(8,128)(2,1)} %all-gather.11.cloned.1.call-done, bf16[1152,2240]{1,0:T(8,128)(2,1)} %copy.13, pred[]{:T(512)S(6)} %eq.2, bf16[1024,2240]{0,1:T(8,128)(2,1)} %param.5, f32[2240]{0:T(1024)S(1)} %copy-done.3, f32[1024]{0:T(1024)S(1)} %add_sqrt_fusion), kind=kOutput, calls=%fused_computation.12 | convolution fusion | flops 5297758208 | bytes 17281792 | tf_op jit(solution)/shard_map/dot_general | solution.py:174
  258.6 5.5 %broadcast_select_fusion = bf16[1152,2240]{1,0:T(8,128)(2,1)} fusion(bf16[1152,2240]{1,0:T(8,128)(2,1)S(1)} %copy-done, bf16[1152,2240]{1,0:T(8,128)(2,1)} %all-gather.11.cloned.1.call-done, pred[]{:T(512)S(6)} %eq.2), kind=kLoop, calls=%fused_computation.8 | loop fusion | flops 2580480 | bytes 15482881 | tf_op jit(solution)/shard_map/jit(_where)/select_n | solution.py:193
  264.1 2.8 copy.16
  266.9 5.7 %shard_map.56 = bf16[1152,1024]{1,0:T(8,128)(2,1)S(1)} custom-call(bf16[1152,1024]{1,0:T(8,128)(2,1)S(1)} %slice_dynamic-update-slice_fusion.q_ref, f32[9,40,128]{2,1,0:T(8,128)S(1)} %pad_maximum_fusion.seen_ref), custom_call_target="tpu_custom_call" | custom-call | flops 1811939328 | bytes 4718592 | tf_op jit(solution)/shard_map/pallas_call | solution.py:128
  272.7 9.4 %add_convert_fusion = bf16[1024,2240]{0,1:T(8,128)(2,1)} fusion(bf16[1024,2240]{0,1:T(8,128)(2,1)} %param.9, bf16[1152,1024]{1,0:T(8,128)(2,1)S(1)} %shard_map.56, bf16[1152,2240]{1,0:T(8,128)(2,1)S(1)} %bitcast.144), kind=kOutput, calls=%fused_computation.5 | convolution fusion | flops 5291704320 | bytes 16695296 | tf_op jit(solution)/shard_map/dot_general | solution.py:201
  (49 shorter events, 0.5 us)
Async XLA Ops:
  6.5 42.8 %all-gather.5.cloned.1.call-start = ((), (), s32[]{:S(2)}) async-start(), calls=%async_computation | async-start | bytes 1658880 | tf_op jit(solution)/shard_map/all_gather | solution.py:68
  7.5 9.8 %collective-permute-start = (bf16[72,2240]{1,0:T(8,128)(2,1)S(1)}, bf16[72,2240]{1,0:T(8,128)(2,1)S(1)}, u32[]{:S(2)}, u32[]{:S(2)}) collective-permute-start(bf16[72,2240]{1,0:T(8,128)(2,1)S(1)} %dynamic-slice_bitcast_fusion), channel_id=1, source_target_pairs={{0,80},{80,0},{1,96},{97,1},{8,72},{72,8},{9,104},{105,9},{16,48},... | collective-permute-start | bytes 967688 | tf_op jit(solution)/shard_map/ppermute | solution.py:164
  19.6 70.2 %all-gather.7.cloned.1.call-start = ((), (), s32[]{:S(2)}) async-start(), calls=%async_computation.1 | async-start | bytes 6635520 | tf_op jit(solution)/shard_map/all_gather | solution.py:69
  49.4 71.3 %all-gather.9.cloned.1.call-start = ((), (), s32[]{:S(2)}) async-start(), calls=%async_computation.2 | async-start | bytes 1658880 | tf_op jit(solution)/shard_map/all_gather | solution.py:68
  98.3 35.2 %collective-permute-start.2 = (bf16[1152,2240]{0,1:T(8,128)(2,1)}, bf16[1152,2240]{0,1:T(8,128)(2,1)}, u32[]{:S(2)}, u32[]{:S(2)}) collective-permute-start(bf16[1152,2240]{0,1:T(8,128)(2,1)} %copy.14), channel_id=1, source_target_pairs={{0,1},{1,0},{2,3},{3,2},{4,5},{5,4},{6,7},{7,6},{8,9},{9,8},{10,11... | collective-permute-start | bytes 15482888 | tf_op jit(solution)/shard_map/ppermute | solution.py:73
  98.9 62.0 %all-gather.11.cloned.1.call-start = ((), (), s32[]{:S(2)}) async-start(), calls=%async_computation.3 | async-start | bytes 6635520 | tf_op jit(solution)/shard_map/all_gather | solution.py:69
  120.7 3.5 %copy-start.3 = (f32[2240]{0:T(1024)S(1)}, f32[2240]{0:T(1024)}, u32[]{:S(2)}) copy-start(f32[2240]{0:T(1024)} %param.6) | copy-start | bytes 26884
  120.7 12.8 %slice-start = ((s8[4587520]{0:T(1024)(128)(4,1)}), s8[4194304]{0:T(1024)(128)(4,1)S(1)}, s32[]{:S(2)}) async-start(s8[4587520]{0:T(1024)(128)(4,1)} %bitcast.145), calls=%async_computation.4 | async-start | bytes 8388608
  124.2 9.3 %slice-start.1 = ((s8[4587520]{0:T(1024)(128)(4,1)}), s8[393216]{0:T(1024)(128)(4,1)S(1)}, s32[]{:S(2)}) async-start(s8[4587520]{0:T(1024)(128)(4,1)} %bitcast.145), calls=%async_computation.5 | async-start | bytes 786432
  142.7 5.2 %copy-start.2 = (bf16[1152,1024]{1,0:T(8,128)(2,1)}, bf16[1152,1024]{1,0:T(8,128)(2,1)S(1)}, u32[]{:S(2)}) copy-start(bf16[1152,1024]{1,0:T(8,128)(2,1)S(1)} %get-tuple-element.7) | copy-start | bytes 7077892
  142.7 5.9 %copy-start.1 = (bf16[1152,1024]{1,0:T(8,128)(2,1)}, bf16[1152,1024]{1,0:T(8,128)(2,1)S(1)}, u32[]{:S(2)}) copy-start(bf16[1152,1024]{1,0:T(8,128)(2,1)S(1)} %get-tuple-element.8) | copy-start | bytes 7077892
  169.5 70.9 %collective-permute-start.1 = (bf16[1152,2240]{0,1:T(8,128)(2,1)}, bf16[1152,2240]{0,1:T(8,128)(2,1)}, u32[]{:S(2)}, u32[]{:S(2)}) collective-permute-start(bf16[1152,2240]{0,1:T(8,128)(2,1)} %copy.12), channel_id=1, source_target_pairs={{0,1},{1,0},{2,3},{3,2},{4,5},{5,4},{6,7},{7,6},{8,9},{9,8},{10,11... | collective-permute-start | bytes 15482888 | tf_op jit(solution)/shard_map/ppermute | solution.py:73
  195.4 1.4 collective-permute-start.3
  196.8 4.4 %collective-permute-start.4 = (f32[5,40,128]{2,1,0:T(8,128)S(1)}, f32[5,40,128]{2,1,0:T(8,128)S(1)}, u32[]{:S(2)}, u32[]{:S(2)}) collective-permute-start(f32[5,40,128]{2,1,0:T(8,128)S(1)} %dynamic-slice_add_fusion), channel_id=1, source_target_pairs={{0,2},{1,3},{2,0},{3,1},{4,6},{5,7},{6,4},{7,5},{8,10},{9,11},{10,... | collective-permute-start | bytes 307208 | tf_op jit(solution)/shard_map/ppermute | solution.py:147
  201.2 5.1 %collective-permute-start.5 = (f32[5,40,128]{2,1,0:T(8,128)S(1)}, f32[5,40,128]{2,1,0:T(8,128)S(1)}, u32[]{:S(2)}, u32[]{:S(2)}) collective-permute-start(f32[5,40,128]{2,1,0:T(8,128)S(1)} %add.60), channel_id=1, source_target_pairs={{0,4},{1,5},{2,6},{3,7},{4,0},{5,1},{6,2},{7,3},{8,12},{9,13},{10,... | collective-permute-start | bytes 307208 | tf_op jit(solution)/shard_map/ppermute | solution.py:147
  206.3 4.8 %collective-permute-start.6 = (f32[5,40,128]{2,1,0:T(8,128)S(1)}, f32[5,40,128]{2,1,0:T(8,128)S(1)}, u32[]{:S(2)}, u32[]{:S(2)}) collective-permute-start(f32[5,40,128]{2,1,0:T(8,128)S(1)} %add.61), channel_id=1, source_target_pairs={{0,8},{8,16},{16,24},{24,32},{32,40},{40,48},{48,56},{56,64},{64,7... | collective-permute-start | bytes 307208 | tf_op jit(solution)/shard_map/ppermute | solution.py:149
  211.2 7.0 %collective-permute-start.7 = (f32[5,40,128]{2,1,0:T(8,128)S(1)}, f32[5,40,128]{2,1,0:T(8,128)S(1)}, u32[]{:S(2)}, u32[]{:S(2)}) collective-permute-start(f32[5,40,128]{2,1,0:T(8,128)S(1)} %add.62), channel_id=1, source_target_pairs={{0,16},{8,24},{16,32},{24,40},{32,48},{40,56},{48,64},{56,72},{64,... | collective-permute-start | bytes 307208 | tf_op jit(solution)/shard_map/ppermute | solution.py:149
  218.2 7.8 %collective-permute-start.8 = (f32[5,40,128]{2,1,0:T(8,128)S(1)}, f32[5,40,128]{2,1,0:T(8,128)S(1)}, u32[]{:S(2)}, u32[]{:S(2)}) collective-permute-start(f32[5,40,128]{2,1,0:T(8,128)S(1)} %add.63), channel_id=1, source_target_pairs={{0,32},{8,40},{16,48},{24,56},{32,64},{40,72},{48,80},{56,88},{64,... | collective-permute-start | bytes 307208 | tf_op jit(solution)/shard_map/ppermute | solution.py:149
  226.0 6.4 %collective-permute-start.9 = (f32[5,40,128]{2,1,0:T(8,128)S(1)}, f32[5,40,128]{2,1,0:T(8,128)S(1)}, u32[]{:S(2)}, u32[]{:S(2)}) collective-permute-start(f32[5,40,128]{2,1,0:T(8,128)S(1)} %add.64), channel_id=1, source_target_pairs={{0,64},{8,72},{16,80},{24,88},{32,96},{40,104},{48,112},{56,120},{... | collective-permute-start | bytes 307208 | tf_op jit(solution)/shard_map/ppermute | solution.py:149
  232.4 7.9 %collective-permute-start.10 = (f32[5,40,128]{2,1,0:T(8,128)S(1)}, f32[5,40,128]{2,1,0:T(8,128)S(1)}, u32[]{:S(2)}, u32[]{:S(2)}) collective-permute-start(f32[5,40,128]{2,1,0:T(8,128)S(1)} %add.65), channel_id=1, source_target_pairs={{0,1},{1,0},{2,3},{3,2},{4,5},{5,4},{6,7},{7,6},{8,9},{9,8},{10,11... | collective-permute-start | bytes 307208 | tf_op jit(solution)/shard_map/ppermute | solution.py:73
  248.9 9.7 %copy-start = (bf16[1152,2240]{1,0:T(8,128)(2,1)S(1)}, bf16[1152,2240]{1,0:T(8,128)(2,1)}, u32[]{:S(2)}) copy-start(bf16[1152,2240]{1,0:T(8,128)(2,1)} %copy.13) | copy-start | bytes 15482884
Sparse Core Ops, SparseCore 0:
  19.7 29.6 all-gather.4
  51.0 38.7 all-gather.6
  99.1 21.5 all-gather.8
  122.2 38.7 all-gather.10

commit v2 on v1

v2 whole, which is shorter than its diff:
```python
import jax
import jax.numpy as jnp
from jax import lax
from jax.experimental import pallas as pl
from jax.experimental.pallas import tpu as pltpu
from jax.sharding import PartitionSpec as P

H = 36
HS = 32
INNER = H * HS
GROUPS = INNER // 128
THIRD = 72
BLOCK = 4 * THIRD
STATE_ROWS = 320
BOTH = ("tm", "space")
F32 = jnp.float32
BF16 = jnp.bfloat16

FIRST = {2: 6, 3: 7, 4: 8, 1: 9, 0: 10}
SECOND = {0: 12, 1: 13, 2: 14, 3: 15, 4: 11}


def device(x, z, y, c):
    return ((x % 4) * 4 + z % 4) * 8 + y * 2 + c


def everywhere(move):
    pairs = []
    for t in range(16):
        x, z = divmod(t, 4)
        for y in range(4):
            for c in range(2):
                pairs.append((device(x, z, y, c), device(*move(x, z, y, c))))
    return pairs


def trade_pairs():
    pairs = []
    at = lambda t, y, c: t * 8 + y * 2 + c
    for y in range(4):
        for d in range(5):
            a, b = FIRST[d], SECOND[d]
            pairs += [
                (at(d, y, 0), at(a, y, 0)),
                (at(a, y, 0), at(d, y, 0)),
                (at(d, y, 1), at(b, y, 0)),
                (at(b, y, 1), at(d, y, 1)),
            ]
    return pairs


def kv_third(t, c):
    if t <= 4:
        return 3 * (FIRST, SECOND)[c][t]
    return 3 * t + 1 + c


KV_AT = {kv_third(t, c): (t // 4, t % 4, c) for t in range(16) for c in range(2)}


def q_third(t):
    if t <= 5:
        return 3 * t
    for d in range(5):
        if FIRST[d] == t:
            return 3 * d + 1
        if SECOND[d] == t:
            return 3 * d + 2


Q_AT = {q_third(t): t for t in range(16)}


def pieces(group):
    row, end, out = 128 * group, 128 * group + 128, []
    while row < end:
        third = row // THIRD
        stop = min(end, THIRD * (third + 1))
        out.append((third, row - THIRD * third, stop - THIRD * third))
        row = stop
    return out


def send(a, move):
    return lax.ppermute(a, BOTH, everywhere(move))


def first_axis(step):
    return lambda x, z, y, c: (x, z + step, y, c) if c == 0 else (x + step, z, y, c)


def second_axis(step):
    return lambda x, z, y, c: (x + step, z, y, c) if c == 0 else (x, z + step, y, c)


def other_core(a):
    return send(a, lambda x, z, y, c: (x, z, y, 1 - c))


def along(core_axes):
    groups = {}
    for t in range(16):
        x, z = divmod(t, 4)
        for y in range(4):
            for c in range(2):
                fixed = z if core_axes[c] == "x" else x
                groups.setdefault((y, c, fixed), []).append(device(x, z, y, c))
    return list(groups.values())


def project_kernel(count, *refs):
    weights, normed_ref, out_ref = refs[:count], refs[count], refs[-1]
    step = pl.program_id(0)
    for n in range(count):

        @pl.when(step == n)
        def _():
            out = jnp.dot(weights[n][...], normed_ref[...], preferred_element_type=F32)
            out_ref[0] = out.astype(BF16).astype(F32)


def project(buffer, normed, blocks):
    places = list(blocks)
    count = len(places)
    depth, rows = normed.shape

    def place(n):
        out = jnp.int32(places[-1])
        for i in range(count - 1):
            out = jnp.where(n == i, places[i], out)
        return out

    kept = [] if buffer is None else [buffer]
    return pl.pallas_call(
        lambda *refs: project_kernel(count, *refs[: count + 1], refs[-1]),
        grid=(count,),
        in_specs=[pl.BlockSpec(memory_space=pltpu.VMEM)] * (count + 1)
        + [pl.BlockSpec(memory_space=pl.ANY)] * len(kept),
        out_specs=pl.BlockSpec((1, BLOCK, rows), lambda n: (place(n), 0, 0)),
        out_shape=jax.ShapeDtypeStruct((8, BLOCK, rows), F32),
        input_output_aliases={count + 1: 0} if kept else {},
        compiler_params=pltpu.CompilerParams(vmem_limit_bytes=28 * 2**20),
        cost_estimate=pl.CostEstimate(
            flops=2 * count * BLOCK * depth * rows, bytes_accessed=count * BLOCK * (2 * depth + 4 * rows), transcendentals=0
        ),
    )(*[blocks[p] for p in places], normed, *kept)


def state_kernel(at_ref, projected_ref, out_ref):
    core, my_x, my_z = at_ref[0], at_ref[1], at_ref[2]
    columns = projected_ref.shape[-1]
    contract = (((1,), (1,)), ((), ()))
    head = lax.broadcasted_iota(jnp.int32, (HS, 128), 1) // HS

    def rows(first_third, group):
        out = []
        for third, start, stop in pieces(group):
            x, z, c = KV_AT[first_third + third]
            dx, dz = (x - my_x) & 3, (z - my_z) & 3
            outer, inner = (dx, dz) if c == 0 else (dz, dx)
            which = core if c == 0 else 1 - core
            out.append(projected_ref[which * 16 + outer * 4 + inner, start:stop, :])
        return jnp.concatenate(out, axis=0)

    out_ref[GROUPS * HS :, :] = jnp.zeros((STATE_ROWS - GROUPS * HS, 128), F32)
    ones = jnp.ones((8, columns), BF16)
    for g in range(GROUPS):
        keys = jnp.maximum(rows(16, g), 0).astype(BF16)
        values = rows(32, g).astype(BF16)
        full = lax.dot_general(keys, values, contract, preferred_element_type=F32)
        state = full[:HS]
        for b in range(1, 4):
            state = jnp.where(head == b, full[b * HS : (b + 1) * HS], state)
        out_ref[g * HS : (g + 1) * HS, :] = state
        norm = lax.dot_general(ones, keys, contract, preferred_element_type=F32)
        out_ref[GROUPS * HS + g : GROUPS * HS + g + 1, :] = norm[:1]


def block_states(at, projected):
    rows = projected.shape[-1]
    return pl.pallas_call(
        state_kernel,
        in_specs=[pl.BlockSpec(memory_space=pltpu.SMEM), pl.BlockSpec(memory_space=pltpu.VMEM)],
        out_specs=pl.BlockSpec(memory_space=pltpu.VMEM),
        out_shape=jax.ShapeDtypeStruct((STATE_ROWS, 128), F32),
        compiler_params=pltpu.CompilerParams(vmem_limit_bytes=28 * 2**20),
        cost_estimate=pl.CostEstimate(flops=2 * 128 * INNER * rows, bytes_accessed=8 * INNER * rows, transcendentals=0),
    )(at, projected.reshape(32, THIRD, rows))


def query_kernel(at_ref, mine_ref, theirs_ref, normed_ref, out_ref):
    core = at_ref[0]

    def run(weights):
        out = jnp.dot(weights[...], normed_ref[...], preferred_element_type=F32)
        out_ref[0] = jnp.maximum(out.astype(BF16), 0).astype(F32)

    @pl.when(core == 0)
    def _():
        run(mine_ref)

    @pl.when(core != 0)
    def _():
        run(theirs_ref)


def project_queries(at, mine, theirs, normed):
    depth, rows = normed.shape
    return pl.pallas_call(
        query_kernel,
        grid_spec=pltpu.PrefetchScalarGridSpec(
            num_scalar_prefetch=1,
            grid=(4,),
            in_specs=[
                pl.BlockSpec((BLOCK, depth), lambda n, at: (jnp.where(at[0] == 0, n, 0), 0)),
                pl.BlockSpec((BLOCK, depth), lambda n, at: (jnp.where(at[0] == 0, 0, n), 0)),
                pl.BlockSpec(memory_space=pltpu.VMEM),
            ],
            out_specs=pl.BlockSpec((1, BLOCK, rows), lambda n, at: (n, 0, 0)),
        ),
        out_shape=jax.ShapeDtypeStruct((4, BLOCK, rows), F32),
        compiler_params=pltpu.CompilerParams(vmem_limit_bytes=28 * 2**20),
        cost_estimate=pl.CostEstimate(
            flops=2 * INNER * depth * rows, bytes_accessed=INNER * (2 * depth + 4 * rows), transcendentals=0
        ),
    )(at, mine, theirs, normed)


def split_dot(a, b):
    high = a.astype(BF16)
    low = (a - high.astype(F32)).astype(BF16)
    return jnp.dot(high, b, preferred_element_type=F32) + jnp.dot(low, b, preferred_element_type=F32)


def out_kernel(at_ref, queries_ref, seen_ref, mine_ref, theirs_ref, ffn_ref, out_ref, wide_ref, attended_ref):
    core = at_ref[0]

    @pl.when(pl.program_id(0) == 0)
    def _():
        same = (
            lax.broadcasted_iota(jnp.int32, (128, 128), 0) // HS
            == lax.broadcasted_iota(jnp.int32, (128, 128), 1) // HS
        )
        for g in range(GROUPS):
            queries = [queries_ref[Q_AT[u], a:b, :] for u, a, b in pieces(g)]
            queries = jnp.concatenate(queries, axis=0).astype(BF16)
            state = seen_ref[g * HS : (g + 1) * HS, :]
            norm = seen_ref[GROUPS * HS + g : GROUPS * HS + g + 1, :]
            state = jnp.where(same, jnp.concatenate([state] * 4, axis=0), 0.0)
            norm = jnp.where(same, jnp.broadcast_to(norm, (128, 128)), 0.0)
            numerator = split_dot(state.T, queries)
            denominator = split_dot(norm, queries) + 1e-06
            result = numerator / denominator
            row = 0
            for t, a, b in pieces(g):
                slot = (t % 4) * 4 + t // 4
                wide_ref[slot * THIRD + a : slot * THIRD + b, :] = result[row : row + b - a]
                row += b - a
        attended_ref[...] = wide_ref[...].astype(BF16)

    def run(weights):
        out = lax.dot_general(
            weights[...], attended_ref[...], (((0,), (0,)), ((), ())), preferred_element_type=F32
        )
        out_ref[...] = (out + ffn_ref[...].astype(F32)).astype(BF16)

    @pl.when(core == 0)
    def _():
        run(theirs_ref)

    @pl.when(core != 0)
    def _():
        run(mine_ref)


def attend_and_mix(at, queries, seen, mine, theirs, ffn):
    depth, rows = ffn.shape
    wide = 512
    return pl.pallas_call(
        out_kernel,
        grid_spec=pltpu.PrefetchScalarGridSpec(
            num_scalar_prefetch=1,
            grid=(pl.cdiv(depth, wide),),
            in_specs=[
                pl.BlockSpec(memory_space=pltpu.VMEM),
                pl.BlockSpec(memory_space=pltpu.VMEM),
                pl.BlockSpec((INNER, wide), lambda n, at: (0, jnp.where(at[0] == 0, 0, n))),
                pl.BlockSpec((INNER, wide), lambda n, at: (0, jnp.where(at[0] == 0, n, 0))),
                pl.BlockSpec((wide, rows), lambda n, at: (n, 0)),
            ],
            out_specs=pl.BlockSpec((wide, rows), lambda n, at: (n, 0)),
            scratch_shapes=[pltpu.VMEM((INNER, rows), F32), pltpu.VMEM((INNER, rows), BF16)],
        ),
        out_shape=jax.ShapeDtypeStruct((depth, rows), BF16),
        compiler_params=pltpu.CompilerParams(vmem_limit_bytes=40 * 2**20),
        cost_estimate=pl.CostEstimate(
            flops=2 * INNER * depth * rows + 8 * 128 * INNER * rows,
            bytes_accessed=INNER * 2 * depth + 4 * depth * rows,
            transcendentals=0,
        ),
    )(at, queries.reshape(16, THIRD, rows), seen, mine, theirs, ffn)


def halves(a, bit):
    size = a.shape[0] // 2
    return lax.dynamic_slice_in_dim(a, bit * size, size, 0), lax.dynamic_slice_in_dim(a, (1 - bit) * size, size, 0)


def swap_bit(a, bit):
    return lax.ppermute(a, "space", [(i, i ^ (1 << bit)) for i in range(8)])


def sum_over_space(state, space):
    part = state.reshape(8, STATE_ROWS // 8, 128)
    for b in range(3):
        keep, give = halves(part, (space >> b) & 1)
        part = keep + swap_bit(give, b)
    return part


def up_to_here(part):
    for step in (1, 2, 4, 8):
        part = part + lax.ppermute(part, "tm", [(t, t + step) for t in range(16 - step)])
    return part


def spread_over_space(part, space):
    for b in (2, 1, 0):
        theirs = swap_bit(part, b)
        low = ((space >> b) & 1) == 0
        part = jnp.where(low, jnp.concatenate([part, theirs]), jnp.concatenate([theirs, part]))
    return part.reshape(STATE_ROWS, 128)


def after_all(*arrays):
    return lax.optimization_barrier(arrays)


def body(tokens, norm_gain, w_qkv, w_out, ffn_cached):
    t, space = lax.axis_index("tm"), lax.axis_index("space")
    core = space & 1
    at = jnp.stack([core, t >> 2, t & 3]).astype(jnp.int32)
    weights = w_qkv.T
    local = lambda j: lax.dynamic_slice_in_dim(weights, THIRD * j, THIRD, 0)

    traded = lax.ppermute(local(jnp.where(t <= 4, 1 + core, 0)), BOTH, trade_pairs())
    own = jnp.where(t <= 4, traded, local(1 + core))
    part_qo = jnp.where(core == 0, jnp.where(t >= 6, traded, weights[:THIRD]), w_out)

    floats = tokens.T.astype(F32)
    root_mean = jnp.sqrt(jnp.mean(floats * floats, axis=0, keepdims=True) + 1e-06)
    normed = (floats / root_mean * norm_gain[:, None]).astype(BF16)
    own, normed = after_all(own, normed)

    before, after = send(own, first_axis(1)), send(own, first_axis(-1))
    far = jnp.concatenate([send(before[:40], first_axis(1)), send(after[40:], first_axis(-1))])
    block = jnp.concatenate([own, after, far, before])
    before, after = send(block, second_axis(1)), send(block, second_axis(-1))
    block_other = other_core(block)
    buffer = project(None, normed, {0: block})
    buffer = project(buffer, normed, {4: block_other})
    before, after, buffer = after_all(before, after, buffer)

    far = jnp.concatenate([send(before[: BLOCK // 2], second_axis(1)), send(after[BLOCK // 2 :], second_axis(-1))])
    before_other, after_other = other_core(before), other_core(after)
    buffer = project(buffer, normed, {1: after, 3: before})
    buffer = project(buffer, normed, {5: after_other, 7: before_other})
    far, buffer = after_all(far, buffer)

    far_other = other_core(far)
    buffer = project(buffer, normed, {2: far})
    buffer = project(buffer, normed, {6: far_other})
    state = block_states(at, buffer)

    part_qo = lax.all_gather(part_qo, BOTH, axis=0, tiled=True, axis_index_groups=along("zx"))
    part_qo, _ = after_all(part_qo, far)
    mine_qo = lax.all_gather(part_qo, BOTH, axis=0, tiled=True, axis_index_groups=along("xz"))

    state = sum_over_space(state, space)
    mine_qo, state = after_all(mine_qo.reshape(16, THIRD, -1), state)
    theirs_qo = other_core(mine_qo).reshape(INNER, -1)
    mine_qo = mine_qo.reshape(INNER, -1)
    queries = project_queries(at, mine_qo, theirs_qo, normed)
    seen = spread_over_space(up_to_here(state), space)
    return attend_and_mix(at, queries, seen, mine_qo, theirs_qo, ffn_cached.T).T


def solution(mesh):
    return jax.shard_map(
        body,
        mesh=mesh,
        in_specs=(
            P(("tm", "space"), None),
            P(),
            P(None, "tm"),
            P("tm", None),
            P(("tm", "space"), None),
        ),
        out_specs=P(("tm", "space"), None),
        check_vma=False,
    )
```

time: 291 us -> 197 us (0.68)
  waiting for transfers between devices: 122 us -> 39.7 us
  matrix products: 37.2 us -> 0 us
  starting transfers between devices: 37.6 us -> 70.1 us
  local copies, waits for them, and re-layouts: 55.2 us -> 26.9 us
  Pallas kernels: 12 us -> 38.9 us
  other arithmetic: 11.3 us -> 7.36 us
    all_gather x4 -> x2, waiting for transfers between devices: 103 us -> 8.21 us  [body(): lax.all_gather(part_qo, BOTH, axis=0, tiled=True, axis_index_groups=along...]
    dot_general x4 -> x0, matrix products: 37.2 us -> none  [the longest x3 27.8 us: body(): jnp.dot(w, normed, preferred_element_type=F32).astype(BF16)]
    ppermute x11 -> x24, starting transfers between devices: 37.5 us -> 70 us  [the longest x13 28.7 us: send(): return lax.ppermute(a, BOTH, everywhere(move))]
    pallas_call x2 -> x9, Pallas kernels: 12 us -> 38.9 us  [the longest x6 15 us: project(): pl.pallas_call(lambda *refs: project_kernel(count, *refs[:count + 1], ref...]
    all_gather x2 -> x0, local copies, waits for them, and re-layouts: 17 us -> none  [gather(): lax.all_gather(part, BOTH, axis=0, tiled=True, axis_index_groups=along('x...]
    ppermute x11 -> x24, waiting for transfers between devices: 18.3 us -> 31.5 us  [the longest x13 19.8 us: send(): return lax.ppermute(a, BOTH, everywhere(move))]
    ppermute x1 -> x0, local copies, waits for them, and re-layouts: 8.53 us -> none  [other_core(): return lax.ppermute(a, 'space', [(i, i ^ 1) for i in range(8)])]
    select_n x4, other arithmetic: 7.67 us -> 0.95 us  [the longest x1 0.93 us: body(): own = jnp.where(t <= 4, traded, local(1 + core))]
  transfers between devices with their start and end apart: 15 -> 26, of which waited for: 13 -> 16; matrix products, arithmetic and copies ran while one was open for 16% -> 4% of each run, Pallas kernels for 2% -> 9%
where the time goes in v2:
time: 197 us
  starting transfers between devices  70.1 us (36%)
  waiting for transfers between devices  39.7 us (20%)
  Pallas kernels  38.9 us (20%)
  local copies, waits for them, and re-layouts  26.9 us (14%)
  between operations  13.8 us (7%)
  other arithmetic  7.36 us (4%)
    ppermute x13, starting transfers between devices, send(): return lax.ppermute(a, BOTH, everywhere(move))  28.7 us
    unnamed x32, local copies, waits for them, and re-layouts  24.4 us
    ppermute x13, waiting for transfers between devices, send(): return lax.ppermute(a, BOTH, everywhere(move))  19.8 us
    ppermute x4, starting transfers between devices, up_to_here(): lax.ppermute(part, 'tm', [(t, t + step) for t in range(16 - step)])  19.2 us
    ppermute x6, starting transfers between devices, swap_bit(): return lax.ppermute(a, 'space', [(i, i ^ 1 << bit) for i in range(8)])  16.2 us
    pallas_call x6, Pallas kernels, project(): pl.pallas_call(lambda *refs: project_kernel(count, *refs[:count + 1], ref...  15 us
    pallas_call x1, Pallas kernels, attend_and_mix(): pl.pallas_call(out_kernel, grid_spec=pltpu.PrefetchScalarGridSpec(num_sca...  13.6 us
    pallas_call x1, Pallas kernels, project_queries(): pl.pallas_call(query_kernel, grid_spec=pltpu.PrefetchScalarGridSpec(num_s...  8.39 us
  transfers between devices with their start and end apart: 26, of which 16 were waited for; matrix products, arithmetic and copies ran while one was open for 4% of the time, Pallas kernels for 9%

profile of v2, /device:TPU:1, one launch (start us, length us, event | category | flops | bytes accessed | tf_op | source)
XLA Modules:
  0.0 196.7 jit_solution(9122555934911508579)
XLA Ops:
  6.5 1.1 dynamic-slice_bitcast_fusion
  7.7 5.9 %collective-permute-start = (bf16[72,2240]{1,0:T(8,128)(2,1)S(1)}, bf16[72,2240]{1,0:T(8,128)(2,1)S(1)}, u32[]{:S(2)}, u32[]{:S(2)}) collective-permute-start(bf16[72,2240]{1,0:T(8,128)(2,1)S(1)} %dynamic-slice_bitcast_fusion), channel_id=1, source_target_pairs={{0,80},{80,0},{1,96},{97,1},{8,72},{72,8},{9,104},{105,9},{16,48},... | collective-permute-start | bytes 967688 | tf_op jit(solution)/shard_map/ppermute | solution.py:346
  13.6 3.3 %fusion = f32[1024]{0:T(1024)S(1)} fusion(bf16[1024,2240]{0,1:T(8,128)(2,1)} %param.5), kind=kLoop, calls=%fused_computation.2 | loop fusion | flops 6880256 | bytes 4591616 | tf_op jit(solution)/shard_map/reduce_sum | solution.py:351
  17.0 2.9 %fusion.3.refs_1_.refs_2_.normed_ref = bf16[2240,1024]{1,0:T(8,128)(2,1)} fusion(bf16[1024,2240]{0,1:T(8,128)(2,1)S(1)} %copy-done.8, f32[2240]{0:T(1024)S(1)} %copy-done.11, f32[1024]{0:T(1024)S(1)} %add_sqrt_fusion), kind=kLoop, calls=%fused_computation.5 | loop fusion | flops 9175040 | bytes 9188096 | tf_op jit(solution)/shard_map/convert_element_type | solution.py:352
  19.9 0.9 bitcast_select_fusion
  20.8 5.4 %collective-permute-start.2 = (bf16[72,2240]{1,0:T(8,128)(2,1)S(1)}, bf16[72,2240]{1,0:T(8,128)(2,1)S(1)}, u32[]{:S(2)}, u32[]{:S(2)}) collective-permute-start(bf16[72,2240]{1,0:T(8,128)(2,1)S(1)} %get-tuple-element.15), channel_id=1, source_target_pairs={{0,8},{1,33},{2,10},{3,35},{4,12},{5,37},{6,14},{7,39},{8,16},{9,4... | collective-permute-start | bytes 967688 | tf_op jit(solution)/shard_map/ppermute | solution.py:85
  26.2 4.0 %collective-permute-done.2 = bf16[72,2240]{1,0:T(8,128)(2,1)S(1)} collective-permute-done((bf16[72,2240]{1,0:T(8,128)(2,1)S(1)}, bf16[72,2240]{1,0:T(8,128)(2,1)S(1)}, u32[]{:S(2)}, u32[]{:S(2)}) %collective-permute-start.2) | collective-permute-done | bytes 322592 | tf_op jit(solution)/shard_map/ppermute | solution.py:85
  30.3 2.2 %collective-permute-start.3 = (bf16[40,2240]{1,0:T(8,128)(2,1)S(1)}, bf16[40,2240]{1,0:T(8,128)(2,1)S(1)}, u32[]{:S(2)}, u32[]{:S(2)}) collective-permute-start(bf16[40,2240]{1,0:T(8,128)(2,1)S(1)} %slice.21), channel_id=1, source_target_pairs={{0,8},{1,33},{2,10},{3,35},{4,12},{5,37},{6,14},{7,39},{8,16},{9,4... | collective-permute-start | bytes 537608 | tf_op jit(solution)/shard_map/ppermute | solution.py:85
  32.5 0.7 collective-permute-start.4
  33.3 2.8 %collective-permute-done.3 = bf16[40,2240]{1,0:T(8,128)(2,1)S(1)} collective-permute-done((bf16[40,2240]{1,0:T(8,128)(2,1)S(1)}, bf16[40,2240]{1,0:T(8,128)(2,1)S(1)}, u32[]{:S(2)}, u32[]{:S(2)}) %collective-permute-start.3) | collective-permute-done | bytes 179232 | tf_op jit(solution)/shard_map/ppermute | solution.py:85
  36.1 0.5 collective-permute-done.4
  36.6 3.4 %collective-permute-start.7 = (bf16[288,2240]{1,0:T(8,128)(2,1)S(1)}, bf16[288,2240]{1,0:T(8,128)(2,1)}, u32[]{:S(2)}, u32[]{:S(2)}) collective-permute-start(bf16[288,2240]{1,0:T(8,128)(2,1)S(1)} %constant_dynamic-update-slice_fusion.refs_0_), channel_id=1, source_target_pairs={{0,1},{1,0},{2,3},{3,2},{4,5},{5,4},{6,7},{7,6},{8,9},{9,8},{10,11... | collective-permute-start | bytes 3870728 | tf_op jit(solution)/shard_map/ppermute | solution.py:85
  40.1 2.7 %collective-permute-start.6 = (bf16[288,2240]{1,0:T(8,128)(2,1)S(1)}, bf16[288,2240]{1,0:T(8,128)(2,1)}, u32[]{:S(2)}, u32[]{:S(2)}) collective-permute-start(bf16[288,2240]{1,0:T(8,128)(2,1)S(1)} %constant_dynamic-update-slice_fusion.refs_0_), channel_id=1, source_target_pairs={{0,96},{1,25},{2,98},{3,27},{4,100},{5,29},{6,102},{7,31},{8,104},... | collective-permute-start | bytes 3870728 | tf_op jit(solution)/shard_map/ppermute | solution.py:85
  42.7 0.0 all-gather.3.cloned.1.call-update
  42.8 0.0 all-gather.5.cloned.1.call-start
  42.8 2.3 %copy-done.4 = bf16[2240,1024]{1,0:T(8,128)(2,1)S(1)} copy-done((bf16[2240,1024]{1,0:T(8,128)(2,1)S(1)}, bf16[2240,1024]{1,0:T(8,128)(2,1)}, u32[]{:S(2)}) %copy-start.4) | copy-done | bytes 4587544
  45.1 1.5 shard_map.55.refs_2_
  46.7 2.9 %shard_map.56.refs_3_ = f32[8,288,1024]{2,1,0:T(8,128)S(1)} custom-call(bf16[288,2240]{1,0:T(8,128)(2,1)} %collective-permute-done.7.refs_0_, bf16[2240,1024]{1,0:T(8,128)(2,1)S(1)} %copy-done.4, f32[8,288,1024]{2,1,0:T(8,128)S(1)} %shard_map.55.refs_2_), custom_call_target="tpu_custom_call", output_to_operand_aliasing={{}: (2, {})} | custom-call | flops 1321205760 | bytes 2469888 | tf_op jit(solution)/shard_map/pallas_call | solution.py:134
  49.5 8.7 %collective-permute-done.5.refs_1_ = bf16[288,2240]{1,0:T(8,128)(2,1)S(1)} collective-permute-done((bf16[288,2240]{1,0:T(8,128)(2,1)S(1)}, bf16[288,2240]{1,0:T(8,128)(2,1)S(1)}, u32[]{:S(2)}, u32[]{:S(2)}) %collective-permute-start.5) | collective-permute-done | bytes 1290272 | tf_op jit(solution)/shard_map/ppermute | solution.py:85
  58.2 7.8 %collective-permute-start.10 = (bf16[288,2240]{1,0:T(8,128)(2,1)}, bf16[288,2240]{1,0:T(8,128)(2,1)S(1)}, u32[]{:S(2)}, u32[]{:S(2)}) collective-permute-start(bf16[288,2240]{1,0:T(8,128)(2,1)} %collective-permute-done.6.refs_0_), channel_id=1, source_target_pairs={{0,1},{1,0},{2,3},{3,2},{4,5},{5,4},{6,7},{7,6},{8,9},{9,8},{10,11... | collective-permute-start | bytes 3870728 | tf_op jit(solution)/shard_map/ppermute | solution.py:85
  66.0 1.1 slice.19
  67.2 0.1 collective-permute-start.8
  67.2 2.8 %collective-permute-start.9 = (bf16[144,2240]{1,0:T(8,128)(2,1)S(1)}, bf16[144,2240]{1,0:T(8,128)(2,1)S(1)}, u32[]{:S(2)}, u32[]{:S(2)}) collective-permute-start(bf16[144,2240]{1,0:T(8,128)(2,1)S(1)} %slice.19), channel_id=1, source_target_pairs={{0,96},{1,25},{2,98},{3,27},{4,100},{5,29},{6,102},{7,31},{8,104},... | collective-permute-start | bytes 1935368 | tf_op jit(solution)/shard_map/ppermute | solution.py:85
  70.1 4.4 %shard_map.57.refs_3_ = f32[8,288,1024]{2,1,0:T(8,128)S(1)} custom-call(bf16[288,2240]{1,0:T(8,128)(2,1)} %collective-permute-done.6.refs_0_, bf16[288,2240]{1,0:T(8,128)(2,1)S(1)} %collective-permute-done.5.refs_1_, bf16[2240,1024]{1,0:T(8,128)(2,1)S(1)} %copy-done.4, f32[8,288,1024]{2,1,0:T(8,128)S(1)} %shard_map.56.refs_3_), custom_call_target="tpu_custom_call", output_to_operand_aliasing={{}: (3, {})} | custom-call | flops 2642411520 | bytes 4939776 | tf_op jit(solution)/shard_map/pallas_call | solution.py:134
  74.5 3.8 %collective-permute-done.8 = bf16[144,2240]{1,0:T(8,128)(2,1)S(1)} collective-permute-done((bf16[144,2240]{1,0:T(8,128)(2,1)S(1)}, bf16[144,2240]{1,0:T(8,128)(2,1)S(1)}, u32[]{:S(2)}, u32[]{:S(2)}) %collective-permute-start.8) | collective-permute-done | bytes 645152 | tf_op jit(solution)/shard_map/ppermute | solution.py:85
  78.3 0.1 pad_maximum_fusion.refs_0_
  78.4 3.1 %shard_map.58.refs_2_ = f32[8,288,1024]{2,1,0:T(8,128)S(1)} custom-call(bf16[288,2240]{1,0:T(8,128)(2,1)S(1)} %collective-permute-done.10.refs_0_, bf16[288,2240]{1,0:T(8,128)(2,1)S(1)} %collective-permute-done.11.refs_1_, bf16[2240,1024]{1,0:T(8,128)(2,1)S(1)} %copy-done.4, f32[8,288,1024]{2,1,0:T(8,128)S(1)} %shard_map.57.refs_3_), custom_call_target="tpu_custom_call", output_to_operand_aliasing={{}: (3, {})} | custom-call | flops 2642411520 | bytes 4939776 | tf_op jit(solution)/shard_map/pallas_call | solution.py:134
  81.5 3.6 %copy-done = f32[8,288,1024]{2,1,0:T(8,128)} copy-done((f32[8,288,1024]{2,1,0:T(8,128)}, f32[8,288,1024]{2,1,0:T(8,128)S(1)}, u32[]{:S(2)}) %copy-start) | copy-done | bytes 9437208
  85.2 0.0 all-gather.5.cloned.1.call-update
  85.2 3.0 %collective-permute-start.12 = (bf16[288,2240]{1,0:T(8,128)(2,1)S(1)}, bf16[288,2240]{1,0:T(8,128)(2,1)S(1)}, u32[]{:S(2)}, u32[]{:S(2)}) collective-permute-start(bf16[288,2240]{1,0:T(8,128)(2,1)S(1)} %pad_maximum_fusion.refs_0_), channel_id=1, source_target_pairs={{0,1},{1,0},{2,3},{3,2},{4,5},{5,4},{6,7},{7,6},{8,9},{9,8},{10,11... | collective-permute-start | bytes 3870728 | tf_op jit(solution)/shard_map/ppermute | solution.py:85
  88.2 0.1 pad_add_fusion.at_ref
  88.3 3.7 %copy-done.1 = f32[8,288,1024]{2,1,0:T(8,128)S(1)} copy-done((f32[8,288,1024]{2,1,0:T(8,128)S(1)}, f32[8,288,1024]{2,1,0:T(8,128)}, u32[]{:S(2)}) %copy-start.1) | copy-done | bytes 9437208
  91.9 2.3 %copy-done.5 = bf16[2240,1024]{1,0:T(8,128)(2,1)S(1)} copy-done((bf16[2240,1024]{1,0:T(8,128)(2,1)S(1)}, bf16[2240,1024]{1,0:T(8,128)(2,1)}, u32[]{:S(2)}) %copy-start.5) | copy-done | bytes 4587544
  94.2 1.5 shard_map.59.refs_2_
  95.8 1.5 shard_map.60
  97.3 4.0 %copy-done.2 = f32[8,288,1024]{2,1,0:T(8,128)} copy-done((f32[8,288,1024]{2,1,0:T(8,128)}, f32[8,288,1024]{2,1,0:T(8,128)S(1)}, u32[]{:S(2)}) %copy-start.2) | copy-done | bytes 9437208
  101.3 3.7 %copy-done.3 = f32[8,288,1024]{2,1,0:T(8,128)S(1)} copy-done((f32[8,288,1024]{2,1,0:T(8,128)S(1)}, f32[8,288,1024]{2,1,0:T(8,128)}, u32[]{:S(2)}) %copy-start.3) | copy-done | bytes 9437208
  105.0 1.9 shard_map.61
  106.9 0.2 collective-permute-start.13
  107.2 1.1 collective-permute-done.13
  108.3 1.5 collective-permute-start.14
  109.8 1.9 collective-permute-done.14
  111.7 3.1 %collective-permute-start.15 = (f32[1,40,128]{2,1,0:T(8,128)S(1)}, f32[1,40,128]{2,1,0:T(8,128)S(1)}, u32[]{:S(2)}, u32[]{:S(2)}) collective-permute-start(f32[1,40,128]{2,1,0:T(8,128)S(1)} %constant_dynamic-slice_fusion), channel_id=1, source_target_pairs={{0,4},{1,5},{2,6},{3,7},{4,0},{5,1},{6,2},{7,3},{8,12},{9,13},{10,... | collective-permute-start | bytes 61448 | tf_op jit(solution)/shard_map/ppermute | solution.py:310
  114.8 1.2 collective-permute-done.15
  116.0 8.2 %all-gather.5.cloned.1.call-done = bf16[1152,2240]{1,0:T(8,128)(2,1)} async-done(((bf16[288,2240]{1,0:T(8,128)(2,1)}), bf16[1152,2240]{1,0:T(8,128)(2,1)}) %all-gather.5.cloned.1.call-update) | async-done | bytes 5160976 | tf_op jit(solution)/shard_map/all_gather | solution.py:377
  124.3 0.6 collective-permute-start.16
  124.8 3.2 %collective-permute-start.17 = (f32[1,40,128]{2,1,0:T(8,128)S(1)}, f32[1,40,128]{2,1,0:T(8,128)S(1)}, u32[]{:S(2)}, u32[]{:S(2)}) collective-permute-start(f32[1,40,128]{2,1,0:T(8,128)S(1)} %dynamic-slice_add_fusion.2), channel_id=1, source_target_pairs={{0,8},{8,16},{16,24},{24,32},{32,40},{40,48},{48,56},{56,64},{64,7... | collective-permute-start | bytes 61448 | tf_op jit(solution)/shard_map/ppermute | solution.py:323
  128.0 0.9 collective-permute-done.17
  128.9 5.2 %collective-permute-start.18 = (f32[1,40,128]{2,1,0:T(8,128)S(1)}, f32[1,40,128]{2,1,0:T(8,128)S(1)}, u32[]{:S(2)}, u32[]{:S(2)}) collective-permute-start(f32[1,40,128]{2,1,0:T(8,128)S(1)} %add.75), channel_id=1, source_target_pairs={{0,16},{8,24},{16,32},{24,40},{32,48},{40,56},{48,64},{56,72},{64,... | collective-permute-start | bytes 61448 | tf_op jit(solution)/shard_map/ppermute | solution.py:323
  134.1 0.9 collective-permute-done.18
  135.0 6.0 %collective-permute-start.19 = (f32[1,40,128]{2,1,0:T(8,128)S(1)}, f32[1,40,128]{2,1,0:T(8,128)S(1)}, u32[]{:S(2)}, u32[]{:S(2)}) collective-permute-start(f32[1,40,128]{2,1,0:T(8,128)S(1)} %add.76), channel_id=1, source_target_pairs={{0,32},{8,40},{16,48},{24,56},{32,64},{40,72},{48,80},{56,88},{64,... | collective-permute-start | bytes 61448 | tf_op jit(solution)/shard_map/ppermute | solution.py:323
  141.0 0.9 collective-permute-done.19
  141.9 4.8 %collective-permute-start.20 = (f32[1,40,128]{2,1,0:T(8,128)S(1)}, f32[1,40,128]{2,1,0:T(8,128)S(1)}, u32[]{:S(2)}, u32[]{:S(2)}) collective-permute-start(f32[1,40,128]{2,1,0:T(8,128)S(1)} %add.77), channel_id=1, source_target_pairs={{0,64},{8,72},{16,80},{24,88},{32,96},{40,104},{48,112},{56,120},{... | collective-permute-start | bytes 61448 | tf_op jit(solution)/shard_map/ppermute | solution.py:323
  146.8 0.9 collective-permute-done.20
  147.7 2.8 %collective-permute-start.21 = (f32[1,40,128]{2,1,0:T(8,128)S(1)}, f32[1,40,128]{2,1,0:T(8,128)S(1)}, u32[]{:S(2)}, u32[]{:S(2)}) collective-permute-start(f32[1,40,128]{2,1,0:T(8,128)S(1)} %add.78), channel_id=1, source_target_pairs={{0,4},{1,5},{2,6},{3,7},{4,0},{5,1},{6,2},{7,3},{8,12},{9,13},{10,... | collective-permute-start | bytes 61448 | tf_op jit(solution)/shard_map/ppermute | solution.py:310
  150.4 1.4 collective-permute-done.21
  151.8 1.2 collective-permute-start.22
  153.0 1.6 collective-permute-done.22
  154.7 7.4 %collective-permute-start.23 = (f32[4,40,128]{2,1,0:T(8,128)S(1)}, f32[4,40,128]{2,1,0:T(8,128)S(1)}, u32[]{:S(2)}, u32[]{:S(2)}) collective-permute-start(f32[4,40,128]{2,1,0:T(8,128)S(1)} %maximum_select_fusion.1), channel_id=1, source_target_pairs={{0,1},{1,0},{2,3},{3,2},{4,5},{5,4},{6,7},{7,6},{8,9},{9,8},{10,11... | collective-permute-start | bytes 245768 | tf_op jit(solution)/shard_map/ppermute | solution.py:310
  162.1 0.9 collective-permute-done.23
  163.0 2.3 %copy-done.6 = bf16[2240,1024]{1,0:T(8,128)(2,1)S(1)} copy-done((bf16[2240,1024]{1,0:T(8,128)(2,1)S(1)}, bf16[2240,1024]{1,0:T(8,128)(2,1)}, u32[]{:S(2)}) %copy-start.6) | copy-done | bytes 4587544
  165.3 2.5 %copy-done.7 = bf16[1152,2240]{1,0:T(8,128)(2,1)S(1)} copy-done((bf16[1152,2240]{1,0:T(8,128)(2,1)S(1)}, bf16[1152,2240]{1,0:T(8,128)(2,1)}, u32[]{:S(2)}) %copy-start.7) | copy-done | bytes 5160984
  167.8 8.4 %shard_map.62 = f32[4,288,1024]{2,1,0:T(8,128)S(1)} custom-call(s32[3]{0:T(128)S(1)} %pad_add_fusion.at_ref, bf16[1152,2240]{1,0:T(8,128)(2,1)S(1)} %copy-done.7, bf16[1152,2240]{1,0:T(8,128)(2,1)} %bitcast.11.theirs_ref, bf16[2240,1024]{1,0:T(8,128)(2,1)S(1)} %copy-done.6), custom_call_target="tpu_custom_call" | custom-call | flops 5284823040 | bytes 9879552 | tf_op jit(solution)/shard_map/pallas_call | solution.py:209
  176.3 13.6 %shard_map.63 = bf16[2240,1024]{1,0:T(8,128)(2,1)} custom-call(s32[3]{0:T(128)S(1)} %pad_add_fusion.at_ref, f32[16,72,1024]{2,1,0:T(8,128)S(1)} %bitcast.21, f32[320,128]{1,0:T(8,128)S(1)} %bitcast.25, bf16[1152,2240]{1,0:T(8,128)(2,1)} %all-gather.5.cloned.1.call-done, bf16[1152,2240]{1,0:T(8,128)(2,1)} %bitcast.11.theirs_ref, bf16[2240,1024]{1,0:T(8,128)(2,1)S(1)} %bitcast.24), custom_call_target="tpu_custom_call" | custom-call | flops 6492782592 | bytes 14336000 | tf_op jit(solution)/shard_map/pallas_call | solution.py:279
  (57 shorter events, 0.4 us)
Async XLA Ops:
  6.5 10.4 %copy-start.11 = (f32[2240]{0:T(1024)S(1)}, f32[2240]{0:T(1024)}, u32[]{:S(2)}) copy-start(f32[2240]{0:T(1024)} %param.6) | copy-start | bytes 26884
  6.5 78.6 %all-gather.3.cloned.1.call-start = ((), (), s32[]{:S(2)}) async-start(), calls=%async_computation | async-start | bytes 1658880 | tf_op jit(solution)/shard_map/all_gather | solution.py:375
  6.5 10.4 %copy-start.8 = (bf16[1024,2240]{0,1:T(8,128)(2,1)S(1)}, bf16[1024,2240]{0,1:T(8,128)(2,1)}, u32[]{:S(2)}) copy-start(bf16[1024,2240]{0,1:T(8,128)(2,1)} %param.5) | copy-start | bytes 13762564
  7.7 12.2 %collective-permute-start = (bf16[72,2240]{1,0:T(8,128)(2,1)S(1)}, bf16[72,2240]{1,0:T(8,128)(2,1)S(1)}, u32[]{:S(2)}, u32[]{:S(2)}) collective-permute-start(bf16[72,2240]{1,0:T(8,128)(2,1)S(1)} %dynamic-slice_bitcast_fusion), channel_id=1, source_target_pairs={{0,80},{80,0},{1,96},{97,1},{8,72},{72,8},{9,104},{105,9},{16,48},... | collective-permute-start | bytes 967688 | tf_op jit(solution)/shard_map/ppermute | solution.py:346
  16.9 2.9 %copy-start.9 = (bf16[2240,216]{0,1:T(8,128)(2,1)S(1)}, bf16[2240,216]{0,1:T(8,128)(2,1)}, u32[]{:S(2)}) copy-start(bf16[2240,216]{0,1:T(8,128)(2,1)} %param.7) | copy-start | bytes 2903044
  16.9 2.9 %copy-start.10 = (bf16[72,2240]{1,0:T(8,128)(2,1)S(1)}, bf16[72,2240]{1,0:T(8,128)(2,1)}, u32[]{:S(2)}) copy-start(bf16[72,2240]{1,0:T(8,128)(2,1)} %param.8) | copy-start | bytes 967684
  20.8 11.7 %collective-permute-start.1 = (bf16[72,2240]{1,0:T(8,128)(2,1)S(1)}, bf16[72,2240]{1,0:T(8,128)(2,1)S(1)}, u32[]{:S(2)}, u32[]{:S(2)}) collective-permute-start(bf16[72,2240]{1,0:T(8,128)(2,1)S(1)} %get-tuple-element.15), channel_id=1, source_target_pairs={{0,24},{1,97},{2,26},{3,99},{4,28},{5,101},{6,30},{7,103},{8,0},{9... | collective-permute-start | bytes 967688 | tf_op jit(solution)/shard_map/ppermute | solution.py:85
  20.8 9.5 %collective-permute-start.2 = (bf16[72,2240]{1,0:T(8,128)(2,1)S(1)}, bf16[72,2240]{1,0:T(8,128)(2,1)S(1)}, u32[]{:S(2)}, u32[]{:S(2)}) collective-permute-start(bf16[72,2240]{1,0:T(8,128)(2,1)S(1)} %get-tuple-element.15), channel_id=1, source_target_pairs={{0,8},{1,33},{2,10},{3,35},{4,12},{5,37},{6,14},{7,39},{8,16},{9,4... | collective-permute-start | bytes 967688 | tf_op jit(solution)/shard_map/ppermute | solution.py:85
  30.3 5.8 %collective-permute-start.3 = (bf16[40,2240]{1,0:T(8,128)(2,1)S(1)}, bf16[40,2240]{1,0:T(8,128)(2,1)S(1)}, u32[]{:S(2)}, u32[]{:S(2)}) collective-permute-start(bf16[40,2240]{1,0:T(8,128)(2,1)S(1)} %slice.21), channel_id=1, source_target_pairs={{0,8},{1,33},{2,10},{3,35},{4,12},{5,37},{6,14},{7,39},{8,16},{9,4... | collective-permute-start | bytes 537608 | tf_op jit(solution)/shard_map/ppermute | solution.py:85
  32.5 4.1 %collective-permute-start.4 = (bf16[32,2240]{1,0:T(8,128)(2,1)S(1)}, bf16[32,2240]{1,0:T(8,128)(2,1)S(1)}, u32[]{:S(2)}, u32[]{:S(2)}) collective-permute-start(bf16[32,2240]{1,0:T(8,128)(2,1)S(1)} %slice.22), channel_id=1, source_target_pairs={{0,24},{1,97},{2,26},{3,99},{4,28},{5,101},{6,30},{7,103},{8,0},{9... | collective-permute-start | bytes 430088 | tf_op jit(solution)/shard_map/ppermute | solution.py:85
  36.6 10.0 %collective-permute-start.7 = (bf16[288,2240]{1,0:T(8,128)(2,1)S(1)}, bf16[288,2240]{1,0:T(8,128)(2,1)}, u32[]{:S(2)}, u32[]{:S(2)}) collective-permute-start(bf16[288,2240]{1,0:T(8,128)(2,1)S(1)} %constant_dynamic-update-slice_fusion.refs_0_), channel_id=1, source_target_pairs={{0,1},{1,0},{2,3},{3,2},{4,5},{5,4},{6,7},{7,6},{8,9},{9,8},{10,11... | collective-permute-start | bytes 3870728 | tf_op jit(solution)/shard_map/ppermute | solution.py:85
  40.1 18.1 %collective-permute-start.5 = (bf16[288,2240]{1,0:T(8,128)(2,1)S(1)}, bf16[288,2240]{1,0:T(8,128)(2,1)S(1)}, u32[]{:S(2)}, u32[]{:S(2)}) collective-permute-start(bf16[288,2240]{1,0:T(8,128)(2,1)S(1)} %constant_dynamic-update-slice_fusion.refs_0_), channel_id=1, source_target_pairs={{0,32},{1,9},{2,34},{3,11},{4,36},{5,13},{6,38},{7,15},{8,40},{9,1... | collective-permute-start | bytes 3870728 | tf_op jit(solution)/shard_map/ppermute | solution.py:85
  40.1 18.1 %collective-permute-start.6 = (bf16[288,2240]{1,0:T(8,128)(2,1)S(1)}, bf16[288,2240]{1,0:T(8,128)(2,1)}, u32[]{:S(2)}, u32[]{:S(2)}) collective-permute-start(bf16[288,2240]{1,0:T(8,128)(2,1)S(1)} %constant_dynamic-update-slice_fusion.refs_0_), channel_id=1, source_target_pairs={{0,96},{1,25},{2,98},{3,27},{4,100},{5,29},{6,102},{7,31},{8,104},... | collective-permute-start | bytes 3870728 | tf_op jit(solution)/shard_map/ppermute | solution.py:85
  42.8 81.5 %all-gather.5.cloned.1.call-start = ((), (), s32[]{:S(2)}) async-start(), calls=%async_computation.1 | async-start | bytes 6635520 | tf_op jit(solution)/shard_map/all_gather | solution.py:377
  42.8 2.3 %copy-start.4 = (bf16[2240,1024]{1,0:T(8,128)(2,1)S(1)}, bf16[2240,1024]{1,0:T(8,128)(2,1)}, u32[]{:S(2)}) copy-start(bf16[2240,1024]{1,0:T(8,128)(2,1)} %fusion.3.refs_1_.refs_2_.normed_ref) | copy-start | bytes 13762564
  58.2 20.2 %collective-permute-start.10 = (bf16[288,2240]{1,0:T(8,128)(2,1)}, bf16[288,2240]{1,0:T(8,128)(2,1)S(1)}, u32[]{:S(2)}, u32[]{:S(2)}) collective-permute-start(bf16[288,2240]{1,0:T(8,128)(2,1)} %collective-permute-done.6.refs_0_), channel_id=1, source_target_pairs={{0,1},{1,0},{2,3},{3,2},{4,5},{5,4},{6,7},{7,6},{8,9},{9,8},{10,11... | collective-permute-start | bytes 3870728 | tf_op jit(solution)/shard_map/ppermute | solution.py:85
  66.0 12.4 %collective-permute-start.11 = (bf16[288,2240]{1,0:T(8,128)(2,1)S(1)}, bf16[288,2240]{1,0:T(8,128)(2,1)S(1)}, u32[]{:S(2)}, u32[]{:S(2)}) collective-permute-start(bf16[288,2240]{1,0:T(8,128)(2,1)S(1)} %collective-permute-done.5.refs_1_), channel_id=1, source_target_pairs={{0,1},{1,0},{2,3},{3,2},{4,5},{5,4},{6,7},{7,6},{8,9},{9,8},{10,11... | collective-permute-start | bytes 3870728 | tf_op jit(solution)/shard_map/ppermute | solution.py:85
  67.2 11.1 %collective-permute-start.8 = (bf16[144,2240]{1,0:T(8,128)(2,1)S(1)}, bf16[144,2240]{1,0:T(8,128)(2,1)S(1)}, u32[]{:S(2)}, u32[]{:S(2)}) collective-permute-start(bf16[144,2240]{1,0:T(8,128)(2,1)S(1)} %slice.18), channel_id=1, source_target_pairs={{0,32},{1,9},{2,34},{3,11},{4,36},{5,13},{6,38},{7,15},{8,40},{9,1... | collective-permute-start | bytes 1935368 | tf_op jit(solution)/shard_map/ppermute | solution.py:85
  67.2 11.0 %collective-permute-start.9 = (bf16[144,2240]{1,0:T(8,128)(2,1)S(1)}, bf16[144,2240]{1,0:T(8,128)(2,1)S(1)}, u32[]{:S(2)}, u32[]{:S(2)}) collective-permute-start(bf16[144,2240]{1,0:T(8,128)(2,1)S(1)} %slice.19), channel_id=1, source_target_pairs={{0,96},{1,25},{2,98},{3,27},{4,100},{5,29},{6,102},{7,31},{8,104},... | collective-permute-start | bytes 1935368 | tf_op jit(solution)/shard_map/ppermute | solution.py:85
  81.5 3.6 %copy-start = (f32[8,288,1024]{2,1,0:T(8,128)}, f32[8,288,1024]{2,1,0:T(8,128)S(1)}, u32[]{:S(2)}) copy-start(f32[8,288,1024]{2,1,0:T(8,128)S(1)} %shard_map.58.refs_2_) | copy-start | bytes 28311556
  85.2 10.6 %collective-permute-start.12 = (bf16[288,2240]{1,0:T(8,128)(2,1)S(1)}, bf16[288,2240]{1,0:T(8,128)(2,1)S(1)}, u32[]{:S(2)}, u32[]{:S(2)}) collective-permute-start(bf16[288,2240]{1,0:T(8,128)(2,1)S(1)} %pad_maximum_fusion.refs_0_), channel_id=1, source_target_pairs={{0,1},{1,0},{2,3},{3,2},{4,5},{5,4},{6,7},{7,6},{8,9},{9,8},{10,11... | collective-permute-start | bytes 3870728 | tf_op jit(solution)/shard_map/ppermute | solution.py:85
  88.3 3.7 %copy-start.1 = (f32[8,288,1024]{2,1,0:T(8,128)S(1)}, f32[8,288,1024]{2,1,0:T(8,128)}, u32[]{:S(2)}) copy-start(f32[8,288,1024]{2,1,0:T(8,128)} %copy-done) | copy-start | bytes 28311556
  91.9 2.3 %copy-start.5 = (bf16[2240,1024]{1,0:T(8,128)(2,1)S(1)}, bf16[2240,1024]{1,0:T(8,128)(2,1)}, u32[]{:S(2)}) copy-start(bf16[2240,1024]{1,0:T(8,128)(2,1)} %fusion.3.refs_1_.refs_2_.normed_ref) | copy-start | bytes 13762564
  97.3 4.0 %copy-start.2 = (f32[8,288,1024]{2,1,0:T(8,128)}, f32[8,288,1024]{2,1,0:T(8,128)S(1)}, u32[]{:S(2)}) copy-start(f32[8,288,1024]{2,1,0:T(8,128)S(1)} %shard_map.60) | copy-start | bytes 28311556
  101.3 3.7 %copy-start.3 = (f32[8,288,1024]{2,1,0:T(8,128)S(1)}, f32[8,288,1024]{2,1,0:T(8,128)}, u32[]{:S(2)}) copy-start(f32[8,288,1024]{2,1,0:T(8,128)} %copy-done.2) | copy-start | bytes 28311556
  105.0 71.3 %slice-start = ((s8[4587520]{0:T(1024)(128)(4,1)}), s8[393216]{0:T(1024)(128)(4,1)S(1)}, s32[]{:S(2)}) async-start(s8[4587520]{0:T(1024)(128)(4,1)} %bitcast.22), calls=%async_computation.2 | async-start | bytes 786432
  106.9 1.4 collective-permute-start.13
  108.3 3.3 %collective-permute-start.14 = (f32[2,40,128]{2,1,0:T(8,128)S(1)}, f32[2,40,128]{2,1,0:T(8,128)S(1)}, u32[]{:S(2)}, u32[]{:S(2)}) collective-permute-start(f32[2,40,128]{2,1,0:T(8,128)S(1)} %constant_dynamic-slice_fusion.1), channel_id=1, source_target_pairs={{0,2},{1,3},{2,0},{3,1},{4,6},{5,7},{6,4},{7,5},{8,10},{9,11},{10,... | collective-permute-start | bytes 122888 | tf_op jit(solution)/shard_map/ppermute | solution.py:310
  111.7 4.4 %collective-permute-start.15 = (f32[1,40,128]{2,1,0:T(8,128)S(1)}, f32[1,40,128]{2,1,0:T(8,128)S(1)}, u32[]{:S(2)}, u32[]{:S(2)}) collective-permute-start(f32[1,40,128]{2,1,0:T(8,128)S(1)} %constant_dynamic-slice_fusion), channel_id=1, source_target_pairs={{0,4},{1,5},{2,6},{3,7},{4,0},{5,1},{6,2},{7,3},{8,12},{9,13},{10,... | collective-permute-start | bytes 61448 | tf_op jit(solution)/shard_map/ppermute | solution.py:310
  124.3 38.8 %collective-permute-start.16 = (bf16[16,72,2240]{2,1,0:T(8,128)(2,1)}, bf16[16,72,2240]{2,1,0:T(8,128)(2,1)}, u32[]{:S(2)}, u32[]{:S(2)}) collective-permute-start(bf16[16,72,2240]{2,1,0:T(8,128)(2,1)} %bitcast.20), channel_id=1, source_target_pairs={{0,1},{1,0},{2,3},{3,2},{4,5},{5,4},{6,7},{7,6},{8,9},{9,8},{10,11... | collective-permute-start | bytes 15482888 | tf_op jit(solution)/shard_map/ppermute | solution.py:85
  124.8 4.1 %collective-permute-start.17 = (f32[1,40,128]{2,1,0:T(8,128)S(1)}, f32[1,40,128]{2,1,0:T(8,128)S(1)}, u32[]{:S(2)}, u32[]{:S(2)}) collective-permute-start(f32[1,40,128]{2,1,0:T(8,128)S(1)} %dynamic-slice_add_fusion.2), channel_id=1, source_target_pairs={{0,8},{8,16},{16,24},{24,32},{32,40},{40,48},{48,56},{56,64},{64,7... | collective-permute-start | bytes 61448 | tf_op jit(solution)/shard_map/ppermute | solution.py:323
  128.9 6.1 %collective-permute-start.18 = (f32[1,40,128]{2,1,0:T(8,128)S(1)}, f32[1,40,128]{2,1,0:T(8,128)S(1)}, u32[]{:S(2)}, u32[]{:S(2)}) collective-permute-start(f32[1,40,128]{2,1,0:T(8,128)S(1)} %add.75), channel_id=1, source_target_pairs={{0,16},{8,24},{16,32},{24,40},{32,48},{40,56},{48,64},{56,72},{64,... | collective-permute-start | bytes 61448 | tf_op jit(solution)/shard_map/ppermute | solution.py:323
  135.0 6.9 %collective-permute-start.19 = (f32[1,40,128]{2,1,0:T(8,128)S(1)}, f32[1,40,128]{2,1,0:T(8,128)S(1)}, u32[]{:S(2)}, u32[]{:S(2)}) collective-permute-start(f32[1,40,128]{2,1,0:T(8,128)S(1)} %add.76), channel_id=1, source_target_pairs={{0,32},{8,40},{16,48},{24,56},{32,64},{40,72},{48,80},{56,88},{64,... | collective-permute-start | bytes 61448 | tf_op jit(solution)/shard_map/ppermute | solution.py:323
  141.9 5.7 %collective-permute-start.20 = (f32[1,40,128]{2,1,0:T(8,128)S(1)}, f32[1,40,128]{2,1,0:T(8,128)S(1)}, u32[]{:S(2)}, u32[]{:S(2)}) collective-permute-start(f32[1,40,128]{2,1,0:T(8,128)S(1)} %add.77), channel_id=1, source_target_pairs={{0,64},{8,72},{16,80},{24,88},{32,96},{40,104},{48,112},{56,120},{... | collective-permute-start | bytes 61448 | tf_op jit(solution)/shard_map/ppermute | solution.py:323
  147.7 4.1 %collective-permute-start.21 = (f32[1,40,128]{2,1,0:T(8,128)S(1)}, f32[1,40,128]{2,1,0:T(8,128)S(1)}, u32[]{:S(2)}, u32[]{:S(2)}) collective-permute-start(f32[1,40,128]{2,1,0:T(8,128)S(1)} %add.78), channel_id=1, source_target_pairs={{0,4},{1,5},{2,6},{3,7},{4,0},{5,1},{6,2},{7,3},{8,12},{9,13},{10,... | collective-permute-start | bytes 61448 | tf_op jit(solution)/shard_map/ppermute | solution.py:310
  151.8 2.9 %collective-permute-start.22 = (f32[2,40,128]{2,1,0:T(8,128)S(1)}, f32[2,40,128]{2,1,0:T(8,128)S(1)}, u32[]{:S(2)}, u32[]{:S(2)}) collective-permute-start(f32[2,40,128]{2,1,0:T(8,128)S(1)} %maximum_select_fusion.2), channel_id=1, source_target_pairs={{0,2},{1,3},{2,0},{3,1},{4,6},{5,7},{6,4},{7,5},{8,10},{9,11},{10,... | collective-permute-start | bytes 122888 | tf_op jit(solution)/shard_map/ppermute | solution.py:310
  154.7 8.3 %collective-permute-start.23 = (f32[4,40,128]{2,1,0:T(8,128)S(1)}, f32[4,40,128]{2,1,0:T(8,128)S(1)}, u32[]{:S(2)}, u32[]{:S(2)}) collective-permute-start(f32[4,40,128]{2,1,0:T(8,128)S(1)} %maximum_select_fusion.1), channel_id=1, source_target_pairs={{0,1},{1,0},{2,3},{3,2},{4,5},{5,4},{6,7},{7,6},{8,9},{9,8},{10,11... | collective-permute-start | bytes 245768 | tf_op jit(solution)/shard_map/ppermute | solution.py:310
  163.0 2.3 %copy-start.6 = (bf16[2240,1024]{1,0:T(8,128)(2,1)S(1)}, bf16[2240,1024]{1,0:T(8,128)(2,1)}, u32[]{:S(2)}) copy-start(bf16[2240,1024]{1,0:T(8,128)(2,1)} %fusion.3.refs_1_.refs_2_.normed_ref) | copy-start | bytes 13762564
  165.3 2.5 %copy-start.7 = (bf16[1152,2240]{1,0:T(8,128)(2,1)S(1)}, bf16[1152,2240]{1,0:T(8,128)(2,1)}, u32[]{:S(2)}) copy-start(bf16[1152,2240]{1,0:T(8,128)(2,1)} %all-gather.5.cloned.1.call-done) | copy-start | bytes 15482884
  167.8 8.4 %slice-start.1 = ((s8[4587520]{0:T(1024)(128)(4,1)}), s8[4194304]{0:T(1024)(128)(4,1)S(1)}, s32[]{:S(2)}) async-start(s8[4587520]{0:T(1024)(128)(4,1)} %bitcast.22), calls=%async_computation.3 | async-start | bytes 8388608
Sparse Core Ops, SparseCore 0:
  42.9 27.3 all-gather.2
  85.3 38.8 all-gather.4

commit v3 on v2

v3 whole, which is shorter than its diff:
```python
import functools

import jax
import jax.numpy as jnp
from jax import lax
from jax.experimental import pallas as pl
from jax.experimental.pallas import tpu as pltpu
from jax.sharding import PartitionSpec as P

H = 36
HS = 32
INNER = H * HS
GROUPS = INNER // 128
THIRD = 72
BLOCK = 4 * THIRD
PIECE = 2 * THIRD
STATE_ROWS = 320
BOTH = ("tm", "space")
F32 = jnp.float32
BF16 = jnp.bfloat16

FIRST = {2: 6, 3: 7, 4: 8, 1: 9, 0: 10}
SECOND = {0: 12, 1: 13, 2: 14, 3: 15, 4: 11}


def device(x, z, y, c):
    return ((x % 4) * 4 + z % 4) * 8 + y * 2 + c


def everywhere(move):
    pairs = []
    for t in range(16):
        x, z = divmod(t, 4)
        for y in range(4):
            for c in range(2):
                pairs.append((device(x, z, y, c), device(*move(x, z, y, c))))
    return pairs


def trade_pairs():
    pairs = []
    at = lambda t, y, c: t * 8 + y * 2 + c
    for y in range(4):
        for d in range(5):
            a, b = FIRST[d], SECOND[d]
            pairs += [
                (at(d, y, 0), at(a, y, 0)),
                (at(a, y, 0), at(d, y, 0)),
                (at(d, y, 1), at(b, y, 0)),
                (at(b, y, 1), at(d, y, 1)),
            ]
    return pairs


def kv_third(t, c):
    if t <= 4:
        return 3 * (FIRST, SECOND)[c][t]
    return 3 * t + 1 + c


KV_AT = {kv_third(t, c): (t // 4, t % 4, c) for t in range(16) for c in range(2)}


def q_third(t):
    if t <= 5:
        return 3 * t
    for d in range(5):
        if FIRST[d] == t:
            return 3 * d + 1
        if SECOND[d] == t:
            return 3 * d + 2


Q_AT = {q_third(t): t for t in range(16)}


def pieces(group):
    row, end, out = 128 * group, 128 * group + 128, []
    while row < end:
        third = row // THIRD
        stop = min(end, THIRD * (third + 1))
        out.append((third, row - THIRD * third, stop - THIRD * third))
        row = stop
    return out


def send(a, move):
    return lax.ppermute(a, BOTH, everywhere(move))


def first_axis(step):
    return lambda x, z, y, c: (x, z + step, y, c) if c == 0 else (x + step, z, y, c)


def second_axis(step):
    return lambda x, z, y, c: (x + step, z, y, c) if c == 0 else (x, z + step, y, c)


def other_core(a):
    return send(a, lambda x, z, y, c: (x, z, y, 1 - c))


def start_all(copies):
    for copy in copies:
        copy.start()
    return copies


def wait_all(copies):
    for copy in copies:
        copy.wait()


def load_weights(sources, weights_ref, sems):
    return [
        pltpu.make_async_copy(source, weights_ref.at[pl.ds(n * PIECE, PIECE)], sems.at[n])
        for n, source in enumerate(sources)
    ]


def load_by_core(at_ref, first, second, weights_ref, sems, act):
    for core, sources in enumerate((first, second)):

        @pl.when(at_ref[0] == core)
        def _():
            act(load_weights(sources, weights_ref, sems))


def project_kernel(places, *refs):
    sources, normed_ref, out_ref = refs[: len(places)], refs[len(places)], refs[-1]
    weights = jnp.concatenate([source[...] for source in sources], axis=0)
    out = jnp.dot(weights, normed_ref[...], preferred_element_type=F32).astype(BF16)
    for n, place in enumerate(places):
        out_ref[place] = out[n * PIECE : (n + 1) * PIECE]


def query_kernel(places, at_ref, *refs):
    count = len(places)
    mine, theirs, normed_ref = refs[:count], refs[count : 2 * count], refs[2 * count]
    out_ref, weights_ref, sems = refs[-3:]
    load_by_core(at_ref, mine, theirs, weights_ref, sems, start_all)
    load_by_core(at_ref, mine, theirs, weights_ref, sems, wait_all)
    out = jnp.dot(weights_ref[...], normed_ref[...], preferred_element_type=F32)
    out = jnp.maximum(out, 0).astype(BF16)
    for n, place in enumerate(places):
        out_ref[place] = out[n * PIECE : (n + 1) * PIECE]


def project_call(kernel, buffer, size, places, smem, sources, source_space, scratch, normed):
    count = len(places)
    depth, rows = normed.shape
    kept = [] if buffer is None else [buffer]
    vmem = pl.BlockSpec(memory_space=pltpu.VMEM)
    return pl.pallas_call(
        functools.partial(kernel, tuple(places)),
        in_specs=[pl.BlockSpec(memory_space=pltpu.SMEM)] * len(smem)
        + [pl.BlockSpec(memory_space=source_space)] * len(sources)
        + [vmem] * (1 + len(kept)),
        out_specs=vmem,
        out_shape=jax.ShapeDtypeStruct((size, PIECE, rows), BF16),
        input_output_aliases={len(smem) + len(sources) + 1: 0} if kept else {},
        scratch_shapes=scratch,
        compiler_params=pltpu.CompilerParams(vmem_limit_bytes=14 * 2**20),
        cost_estimate=pl.CostEstimate(
            flops=2 * count * PIECE * depth * rows, bytes_accessed=count * PIECE * 2 * (depth + rows), transcendentals=0
        ),
    )(*smem, *sources, normed, *kept)


def project(buffer, normed, places):
    return project_call(project_kernel, buffer, 16, places, [], list(places.values()), pltpu.VMEM, [], normed)


def project_queries(buffer, at, normed, places):
    sources = [mine for mine, _ in places.values()] + [theirs for _, theirs in places.values()]
    count = len(places)
    scratch = [pltpu.VMEM((count * PIECE, normed.shape[0]), BF16), pltpu.SemaphoreType.DMA((count,))]
    return project_call(query_kernel, buffer, 8, places, [at], sources, pl.ANY, scratch, normed)


def state_kernel(at_ref, projected_ref, out_ref):
    core, my_x, my_z = at_ref[0], at_ref[1], at_ref[2]
    columns = projected_ref.shape[-1]
    contract = (((1,), (1,)), ((), ()))
    head = lax.broadcasted_iota(jnp.int32, (HS, 128), 1) // HS

    def rows(first_third, group):
        out = []
        for third, start, stop in pieces(group):
            x, z, c = KV_AT[first_third + third]
            dx, dz = (x - my_x) & 3, (z - my_z) & 3
            outer, inner = (dx, dz) if c == 0 else (dz, dx)
            which = core if c == 0 else 1 - core
            out.append(projected_ref[which * 16 + outer * 4 + inner].astype(F32)[start:stop])
        return jnp.concatenate(out, axis=0)

    out_ref[GROUPS * HS :, :] = jnp.zeros((STATE_ROWS - GROUPS * HS, 128), F32)
    ones = jnp.ones((8, columns), BF16)
    for g in range(GROUPS):
        keys = jnp.maximum(rows(16, g), 0).astype(BF16)
        values = rows(32, g).astype(BF16)
        full = lax.dot_general(keys, values, contract, preferred_element_type=F32)
        state = full[:HS]
        for b in range(1, 4):
            state = jnp.where(head == b, full[b * HS : (b + 1) * HS], state)
        out_ref[g * HS : (g + 1) * HS, :] = state
        norm = lax.dot_general(ones, keys, contract, preferred_element_type=F32)
        out_ref[GROUPS * HS + g : GROUPS * HS + g + 1, :] = norm[:1]


def block_states(at, projected):
    rows = projected.shape[-1]
    vmem = pl.BlockSpec(memory_space=pltpu.VMEM)
    return pl.pallas_call(
        state_kernel,
        in_specs=[pl.BlockSpec(memory_space=pltpu.SMEM), vmem],
        out_specs=vmem,
        out_shape=jax.ShapeDtypeStruct((STATE_ROWS, 128), F32),
        compiler_params=pltpu.CompilerParams(vmem_limit_bytes=14 * 2**20),
        cost_estimate=pl.CostEstimate(flops=2 * 128 * INNER * rows, bytes_accessed=4 * INNER * rows, transcendentals=0),
    )(at, projected.reshape(32, THIRD, rows))


def split(a):
    high = a.astype(BF16)
    return jnp.concatenate([high, (a - high.astype(F32)).astype(BF16)], axis=1)


def out_kernel(at_ref, queries_ref, seen_ref, *refs):
    mine, theirs, (ffn_ref, out_ref) = refs[:8], refs[8:16], refs[16:18]
    thirds_ref, wide_ref, attended_ref, weights_ref, ffn_vmem, out_vmem = refs[18:24]
    query_sems, weight_sems, ffn_sems, out_sems = refs[24:]
    core, my_x, my_z = at_ref[0], at_ref[1], at_ref[2]
    depth = out_ref.shape[0]
    parts = [(first, min(512, depth - first)) for first in range(0, depth, 512)]

    query_copy = pltpu.make_async_copy(queries_ref, thirds_ref, query_sems.at[0])
    query_copy.start()
    load_by_core(at_ref, theirs, mine, weights_ref, weight_sems, start_all)
    ffn_copies = [
        pltpu.make_async_copy(ffn_ref.at[pl.ds(f, size)], ffn_vmem.at[pl.ds(f, size)], ffn_sems.at[n])
        for n, (f, size) in enumerate(parts)
    ]
    for copy in ffn_copies:
        copy.start()

    same = (
        lax.broadcasted_iota(jnp.int32, (128, 128), 0) // HS == lax.broadcasted_iota(jnp.int32, (128, 128), 1) // HS
    )
    query_copy.wait()
    for g in range(GROUPS):
        queries = []
        for u, a, b in pieces(g):
            dx, dz = (Q_AT[u] // 4 - my_x) & 3, (Q_AT[u] % 4 - my_z) & 3
            queries.append(thirds_ref[dx * 4 + dz].astype(F32)[a:b])
        queries = jnp.concatenate(queries, axis=0).astype(BF16)
        state = seen_ref[g * HS : (g + 1) * HS, :]
        norm = seen_ref[GROUPS * HS + g : GROUPS * HS + g + 1, :]
        state = jnp.where(same, jnp.concatenate([state] * 4, axis=0), 0.0)
        norm = jnp.where(same, jnp.broadcast_to(norm, (128, 128)), 0.0)
        both = split(jnp.concatenate([state.T, norm], axis=0))
        both = jnp.dot(both, jnp.concatenate([queries, queries], axis=0), preferred_element_type=F32)
        result = both[:128] / (both[128:] + 1e-06)
        row = 0
        for t, a, b in pieces(g):
            dx, dz = (t // 4 - my_x) & 3, (t % 4 - my_z) & 3
            wide_ref[dz * 4 + dx, a:b, :] = result[row : row + b - a]
            row += b - a
    attended_ref[...] = wide_ref[...].reshape(attended_ref.shape).astype(BF16)

    load_by_core(at_ref, theirs, mine, weights_ref, weight_sems, wait_all)
    out_copies = []
    for n, (f, size) in enumerate(parts):
        out = lax.dot_general(
            weights_ref[:, f : f + size], attended_ref[...], (((0,), (0,)), ((), ())), preferred_element_type=F32
        )
        ffn_copies[n].wait()
        out_vmem[f : f + size, :] = (out + ffn_vmem[f : f + size, :].astype(F32)).astype(BF16)
        copy = pltpu.make_async_copy(out_vmem.at[pl.ds(f, size)], out_ref.at[pl.ds(f, size)], out_sems.at[n])
        copy.start()
        out_copies.append(copy)
    for copy in out_copies:
        copy.wait()


def attend_and_mix(at, queries, seen, mine, theirs, ffn):
    depth, rows = ffn.shape
    vmem, hbm = pl.BlockSpec(memory_space=pltpu.VMEM), pl.BlockSpec(memory_space=pltpu.HBM)
    parts = pl.cdiv(depth, 512)
    return pl.pallas_call(
        out_kernel,
        in_specs=[pl.BlockSpec(memory_space=pltpu.SMEM), hbm, vmem] + [hbm] * 17,
        out_specs=hbm,
        out_shape=jax.ShapeDtypeStruct((depth, rows), BF16),
        scratch_shapes=[
            pltpu.VMEM((16, THIRD, rows), BF16),
            pltpu.VMEM((16, THIRD, rows), F32),
            pltpu.VMEM((INNER, rows), BF16),
            pltpu.VMEM((INNER, depth), BF16),
            pltpu.VMEM((depth, rows), BF16),
            pltpu.VMEM((depth, rows), BF16),
            pltpu.SemaphoreType.DMA((1,)),
            pltpu.SemaphoreType.DMA((8,)),
            pltpu.SemaphoreType.DMA((parts,)),
            pltpu.SemaphoreType.DMA((parts,)),
        ],
        compiler_params=pltpu.CompilerParams(vmem_limit_bytes=40 * 2**20),
        cost_estimate=pl.CostEstimate(
            flops=2 * INNER * depth * rows + 8 * 128 * INNER * rows,
            bytes_accessed=INNER * 2 * depth + 4 * depth * rows,
            transcendentals=0,
        ),
    )(at, queries.reshape(16, THIRD, rows), seen, *mine, *theirs, ffn)


def swap_bit(a, bit):
    return lax.ppermute(a, "space", [(i, i ^ (1 << bit)) for i in range(8)])


def sum_over_bit(part, place, b):
    size = part.shape[0] // 2
    half = lambda start: lax.dynamic_slice(
        part, (start, 0, 0), (size,) + part.shape[1:], allow_negative_indices=False
    )
    return half(place["keep"][b]) + swap_bit(half(place["give"][b]), b)


def up_to_here(part):
    for step in (1, 2, 4, 8):
        part = part + lax.ppermute(part, "tm", [(t, t + step) for t in range(16 - step)])
    return part


def spread_over_space(part, place):
    for b in (2, 1, 0):
        theirs = swap_bit(part, b)
        part = jnp.where(place["low"][b], jnp.concatenate([part, theirs]), jnp.concatenate([theirs, part]))
    return part.reshape(STATE_ROWS, 128)


def after_all(*arrays):
    return lax.optimization_barrier(arrays)


def body(tokens, norm_gain, w_qkv, w_out, ffn_cached):
    t, space = lax.axis_index("tm"), lax.axis_index("space")
    core = space & 1
    at = jnp.stack([core, t >> 2, t & 3]).astype(jnp.int32)
    weights = w_qkv.T
    local = lambda j: lax.dynamic_slice_in_dim(weights, THIRD * j, THIRD, 0)

    traded = lax.ppermute(local(jnp.where(t <= 4, 1 + core, 0)), BOTH, trade_pairs())
    own_kv = jnp.where(t <= 4, traded, local(1 + core))
    own_qo = jnp.where(core == 0, jnp.where(t >= 6, traded, weights[:THIRD]), w_out)
    own = jnp.concatenate([own_kv, own_qo])

    floats = tokens.T.astype(F32)
    root_mean = jnp.sqrt(jnp.mean(floats * floats, axis=0, keepdims=True) + 1e-06)
    normed = (floats / root_mean * norm_gain[:, None]).astype(BF16)
    bits = [(space >> b) & 1 for b in range(3)]
    place = dict(
        keep=[bits[b] * (4 >> b) for b in range(3)],
        give=[(1 - bits[b]) * (4 >> b) for b in range(3)],
        low=[bits[b] == 0 for b in range(3)],
    )
    own, normed, at, place = lax.optimization_barrier((own, normed, at, place))

    before, after = send(own, first_axis(1)), send(own, first_axis(-1))
    far_kv, far_qo = send(before[:THIRD], first_axis(1)), send(after[THIRD:], first_axis(-1))
    low = jnp.concatenate([own[:THIRD], after[:THIRD]])
    high = jnp.concatenate([far_kv, before[:THIRD]])
    low_qo = jnp.concatenate([own[THIRD:], after[THIRD:]])
    high_qo = jnp.concatenate([far_qo, before[THIRD:]])

    before_low, after_low = send(low, second_axis(1)), send(low, second_axis(-1))
    before_high, after_high = send(high, second_axis(1)), send(high, second_axis(-1))
    buffer = project(None, normed, {0: low, 1: high, 8: other_core(low), 9: other_core(high)})
    before_low, after_low, buffer = after_all(before_low, after_low, buffer)
    far_low = send(before_low, second_axis(1))
    other = {10: other_core(after_low), 14: other_core(before_low)}
    buffer = project(buffer, normed, {2: after_low, 6: before_low, **other})
    after_high, before_high, buffer, low_qo, high_qo = after_all(after_high, before_high, buffer, low_qo, high_qo)
    far_high = send(after_high, second_axis(-1))
    other = {11: other_core(after_high), 15: other_core(before_high)}

    before_low, after_high_qo = send(low_qo, second_axis(1)), send(high_qo, second_axis(-1))
    mine = [low_qo, high_qo, None, None, None, None, None, None]
    theirs = [other_core(a) for a in mine[:2]] + [None] * 6
    both = lambda places: {p: (mine[p], theirs[p]) for p in places}
    buffer = project(buffer, normed, {3: after_high, 7: before_high, **other})
    queries = project_queries(None, at, normed, both((0, 1)))
    far_low, far_high, buffer, queries = after_all(far_low, far_high, buffer, queries)
    far_low_other, far_high_other = other_core(far_low), other_core(far_high)
    before_high, after_low = send(high_qo, second_axis(1)), send(low_qo, second_axis(-1))
    buffer = project(buffer, normed, {4: far_low, 5: far_high})
    buffer = project(buffer, normed, {12: far_low_other, 13: far_high_other})

    state = block_states(at, buffer).reshape(8, STATE_ROWS // 8, 128)
    state = sum_over_bit(state, place, 0)
    mine[3], mine[6], state = after_all(after_high_qo, before_low, state)
    mine[4], mine[5] = send(mine[6], second_axis(1)), send(mine[3], second_axis(-1))
    theirs[3], theirs[6] = other_core(mine[3]), other_core(mine[6])
    state = sum_over_bit(state, place, 1)
    mine[2], mine[7], state = after_all(after_low, before_high, state)
    theirs[2], theirs[7] = other_core(mine[2]), other_core(mine[7])
    state = sum_over_bit(state, place, 2)
    queries = project_queries(queries, at, normed, both((3, 6, 2, 7)))
    mine[4], mine[5], state, queries = after_all(mine[4], mine[5], state, queries)
    theirs[4], theirs[5] = other_core(mine[4]), other_core(mine[5])
    queries = project_queries(queries, at, normed, both((4, 5)))
    state = up_to_here(state)
    state, queries = after_all(state, queries)
    seen = spread_over_space(state, place)
    return attend_and_mix(at, queries, seen, mine, theirs, ffn_cached.T).T


def solution(mesh):
    return jax.shard_map(
        body,
        mesh=mesh,
        in_specs=(
            P(("tm", "space"), None),
            P(),
            P(None, "tm"),
            P("tm", None),
            P(("tm", "space"), None),
        ),
        out_specs=P(("tm", "space"), None),
        check_vma=False,
    )
```

time: 197 us -> 173 us (0.88)
  local copies, waits for them, and re-layouts: 26.9 us -> 1.32 us
  starting transfers between devices: 70.1 us -> 85.7 us
  between operations: 13.8 us -> 0.53 us
  Pallas kernels: 38.9 us -> 36.5 us
    unnamed x32 -> x10, local copies, waits for them, and re-layouts: 24.4 us -> 0.03 us
    ppermute x13 -> x32, starting transfers between devices: 28.7 us -> 43.5 us  [send(): return lax.ppermute(a, BOTH, everywhere(move))]
    ppermute x13 -> x32, waiting for transfers between devices: 19.8 us -> 31.5 us  [send(): return lax.ppermute(a, BOTH, everywhere(move))]
    all_gather x2 -> x0, waiting for transfers between devices: 8.21 us -> none  [body(): lax.all_gather(part_qo, BOTH, axis=0, tiled=True, axis_index_groups=along...]
    pallas_call x8 -> x9, Pallas kernels: 37 us -> 34.6 us  [the longest x8 21.7 us: project_call(): pl.pallas_call(functools.partial(kernel, tuple(places)), in_specs=[pl.Blo...]
  transfers between devices with their start and end apart: 26 -> 43, of which waited for: 16 -> 22; matrix products, arithmetic and copies ran while one was open for 4% -> 4% of each run, Pallas kernels for 9% -> 12%
where the time goes in v3:
time: 173 us; the launch traced here: 172 us
  starting transfers between devices  85.7 us (50%)
  waiting for transfers between devices  41.4 us (24%)
  Pallas kernels  36.5 us (21%)
  other arithmetic  6.8 us (4%)
    ppermute x32, starting transfers between devices, send(): return lax.ppermute(a, BOTH, everywhere(move))  43.5 us
    ppermute x32, waiting for transfers between devices, send(): return lax.ppermute(a, BOTH, everywhere(move))  31.5 us
    pallas_call x8, Pallas kernels, project_call(): pl.pallas_call(functools.partial(kernel, tuple(places)), in_specs=[pl.Blo...  21.7 us
    ppermute x4, starting transfers between devices, up_to_here(): lax.ppermute(part, 'tm', [(t, t + step) for t in range(16 - step)])  19.7 us
    ppermute x6, starting transfers between devices, swap_bit(): return lax.ppermute(a, 'space', [(i, i ^ 1 << bit) for i in range(8)])  16.6 us
    pallas_call x1, Pallas kernels, attend_and_mix(): pl.pallas_call(out_kernel, in_specs=[pl.BlockSpec(memory_space=pltpu.SMEM...  12.9 us
    ppermute x6, waiting for transfers between devices, swap_bit(): return lax.ppermute(a, 'space', [(i, i ^ 1 << bit) for i in range(8)])  6.43 us
    ppermute x1, starting transfers between devices, body(): lax.ppermute(local(jnp.where(t <= 4, 1 + core, 0)), BOTH, trade_pairs())  5.91 us
  transfers between devices with their start and end apart: 43, of which 22 were waited for; matrix products, arithmetic and copies ran while one was open for 4% of the time, Pallas kernels for 12%

profile of v3, /device:TPU:1, one launch (start us, length us, event | category | flops | bytes accessed | tf_op | source)
XLA Modules:
  0.0 172.3 jit_solution(4588806304457644723)
XLA Ops:
  0.0 1.1 dynamic-slice_bitcast_fusion
  1.2 5.9 %collective-permute-start = (bf16[72,2240]{1,0:T(8,128)(2,1)S(1)}, bf16[72,2240]{1,0:T(8,128)(2,1)S(1)}, u32[]{:S(2)}, u32[]{:S(2)}) collective-permute-start(bf16[72,2240]{1,0:T(8,128)(2,1)S(1)} %dynamic-slice_bitcast_fusion), channel_id=1, source_target_pairs={{0,80},{80,0},{1,96},{97,1},{8,72},{72,8},{9,104},{105,9},{16,48},... | collective-permute-start | bytes 967688 | tf_op jit(solution)/shard_map/ppermute | solution.py:352
  7.1 3.3 %fusion = f32[1024]{0:T(1024)S(1)} fusion(bf16[1024,2240]{0,1:T(8,128)(2,1)} %param.5), kind=kLoop, calls=%fused_computation.2 | loop fusion | flops 6880256 | bytes 4591616 | tf_op jit(solution)/shard_map/reduce_sum | solution.py:358
  10.4 2.9 %fusion.3.refs_4_.refs_2_.refs_8_ = bf16[2240,1024]{1,0:T(8,128)(2,1)} fusion(bf16[1024,2240]{0,1:T(8,128)(2,1)S(1)} %copy-done.1, f32[2240]{0:T(1024)S(1)} %copy-done.4, f32[1024]{0:T(1024)S(1)} %add_sqrt_fusion), kind=kLoop, calls=%fused_computation.5 | loop fusion | flops 9175040 | bytes 9188096 | tf_op jit(solution)/shard_map/convert_element_type | solution.py:359
  13.8 5.4 %collective-permute-start.1 = (bf16[144,2240]{1,0:T(8,128)(2,1)S(1)}, bf16[144,2240]{1,0:T(8,128)(2,1)S(1)}, u32[]{:S(2)}, u32[]{:S(2)}) collective-permute-start(bf16[144,2240]{1,0:T(8,128)(2,1)S(1)} %pad_maximum_fusion), channel_id=1, source_target_pairs={{0,8},{1,33},{2,10},{3,35},{4,12},{5,37},{6,14},{7,39},{8,16},{9,4... | collective-permute-start | bytes 1935368 | tf_op jit(solution)/shard_map/ppermute | solution.py:88
  19.2 7.6 %collective-permute-done.1 = bf16[144,2240]{1,0:T(8,128)(2,1)S(1)} collective-permute-done((bf16[144,2240]{1,0:T(8,128)(2,1)S(1)}, bf16[144,2240]{1,0:T(8,128)(2,1)S(1)}, u32[]{:S(2)}, u32[]{:S(2)}) %collective-permute-start.1) | collective-permute-done | bytes 645152 | tf_op jit(solution)/shard_map/ppermute | solution.py:88
  26.8 2.1 %collective-permute-start.2 = (bf16[72,2240]{1,0:T(8,128)(2,1)S(1)}, bf16[72,2240]{1,0:T(8,128)(2,1)S(1)}, u32[]{:S(2)}, u32[]{:S(2)}) collective-permute-start(bf16[72,2240]{1,0:T(8,128)(2,1)S(1)} %get-tuple-element.78), channel_id=1, source_target_pairs={{0,8},{1,33},{2,10},{3,35},{4,12},{5,37},{6,14},{7,39},{8,16},{9,4... | collective-permute-start | bytes 967688 | tf_op jit(solution)/shard_map/ppermute | solution.py:88
  29.1 1.6 collective-permute-start.8
  30.7 3.7 %collective-permute-done.2 = bf16[72,2240]{1,0:T(8,128)(2,1)S(1)} collective-permute-done((bf16[72,2240]{1,0:T(8,128)(2,1)S(1)}, bf16[72,2240]{1,0:T(8,128)(2,1)S(1)}, u32[]{:S(2)}, u32[]{:S(2)}) %collective-permute-start.2) | collective-permute-done | bytes 322592 | tf_op jit(solution)/shard_map/ppermute | solution.py:88
  34.5 3.8 %collective-permute-start.9 = (bf16[144,2240]{1,0:T(8,128)(2,1)S(1)}, bf16[144,2240]{1,0:T(8,128)(2,1)S(1)}, u32[]{:S(2)}, u32[]{:S(2)}) collective-permute-start(bf16[144,2240]{1,0:T(8,128)(2,1)S(1)} %pad_maximum_fusion.1.refs_1_), channel_id=1, source_target_pairs={{0,1},{1,0},{2,3},{3,2},{4,5},{5,4},{6,7},{7,6},{8,9},{9,8},{10,11... | collective-permute-start | bytes 1935368 | tf_op jit(solution)/shard_map/ppermute | solution.py:88
  38.3 2.7 %collective-permute-start.7 = (bf16[144,2240]{1,0:T(8,128)(2,1)S(1)}, bf16[144,2240]{1,0:T(8,128)(2,1)S(1)}, u32[]{:S(2)}, u32[]{:S(2)}) collective-permute-start(bf16[144,2240]{1,0:T(8,128)(2,1)S(1)} %pad_maximum_fusion.2.refs_0_), channel_id=1, source_target_pairs={{0,96},{1,25},{2,98},{3,27},{4,100},{5,29},{6,102},{7,31},{8,104},... | collective-permute-start | bytes 1935368 | tf_op jit(solution)/shard_map/ppermute | solution.py:88
  40.9 1.5 collective-permute-start.12
  42.4 1.5 collective-permute-start.4
  43.9 2.9 %shard_map.55.refs_5_ = bf16[16,144,1024]{2,1,0:T(8,128)(2,1)S(1)} custom-call(bf16[144,2240]{1,0:T(8,128)(2,1)S(1)} %pad_maximum_fusion.2.refs_0_, bf16[144,2240]{1,0:T(8,128)(2,1)S(1)} %pad_maximum_fusion.1.refs_1_, bf16[144,2240]{1,0:T(8,128)(2,1)S(1)} %collective-permute-done.8.refs_2_, bf16[144,2240]{1,0:T(8,128)(2,1)S(1)} %collective-permute-done.9.refs_3_, ...), custom_call_target="tpu_custom_call" | custom-call | flops 2642411520 | bytes 3760128 | tf_op jit(solution)/shard_map/pallas_call | solution.py:154
  46.8 2.4 %collective-permute-done.6.refs_1_ = bf16[144,2240]{1,0:T(8,128)(2,1)S(1)} collective-permute-done((bf16[144,2240]{1,0:T(8,128)(2,1)S(1)}, bf16[144,2240]{1,0:T(8,128)(2,1)S(1)}, u32[]{:S(2)}, u32[]{:S(2)}) %collective-permute-start.6) | collective-permute-done | bytes 645152 | tf_op jit(solution)/shard_map/ppermute | solution.py:88
  49.3 2.8 %collective-permute-done.7.refs_0_ = bf16[144,2240]{1,0:T(8,128)(2,1)S(1)} collective-permute-done((bf16[144,2240]{1,0:T(8,128)(2,1)S(1)}, bf16[144,2240]{1,0:T(8,128)(2,1)S(1)}, u32[]{:S(2)}, u32[]{:S(2)}) %collective-permute-start.7) | collective-permute-done | bytes 645152 | tf_op jit(solution)/shard_map/ppermute | solution.py:88
  52.1 2.6 %collective-permute-start.10 = (bf16[144,2240]{1,0:T(8,128)(2,1)S(1)}, bf16[144,2240]{1,0:T(8,128)(2,1)S(1)}, u32[]{:S(2)}, u32[]{:S(2)}) collective-permute-start(bf16[144,2240]{1,0:T(8,128)(2,1)S(1)} %collective-permute-done.7.refs_0_), channel_id=1, source_target_pairs={{0,1},{1,0},{2,3},{3,2},{4,5},{5,4},{6,7},{7,6},{8,9},{9,8},{10,11... | collective-permute-start | bytes 1935368 | tf_op jit(solution)/shard_map/ppermute | solution.py:88
  54.8 1.6 collective-permute-done.10.refs_2_
  56.4 0.9 collective-permute-done.11.refs_3_
  57.4 2.9 %shard_map.56.refs_5_ = bf16[16,144,1024]{2,1,0:T(8,128)(2,1)S(1)} custom-call(bf16[144,2240]{1,0:T(8,128)(2,1)S(1)} %collective-permute-done.7.refs_0_, bf16[144,2240]{1,0:T(8,128)(2,1)S(1)} %collective-permute-done.6.refs_1_, bf16[144,2240]{1,0:T(8,128)(2,1)S(1)} %collective-permute-done.10.refs_2_, ...), custom_call_target="tpu_custom_call", output_to_operand_aliasing={{}: (5, {})} | custom-call | flops 2642411520 | bytes 3760128 | tf_op jit(solution)/shard_map/pallas_call | solution.py:154
  60.3 1.5 collective-permute-start.19
  61.8 0.5 collective-permute-start.17
  62.3 1.2 collective-permute-done.19.refs_2_.refs_8_
  63.5 1.5 collective-permute-start.16
  65.0 2.8 %shard_map.58.refs_9_ = bf16[8,144,1024]{2,1,0:T(8,128)(2,1)S(1)} custom-call(s32[3]{0:T(128)S(1)} %pad_add_fusion.at_ref, bf16[144,2240]{1,0:T(8,128)(2,1)S(1)} %pad_maximum_fusion.3.refs_0_, bf16[144,2240]{1,0:T(8,128)(2,1)S(1)} %pad_maximum_fusion.4.refs_1_, bf16[144,2240]{1,0:T(8,128)(2,1)S(1)} %collective-permute-done.19.refs_2_.refs_8_, ...), custom_call_target="tpu_custom_call" | custom-call | flops 1321205760 | bytes 1880064 | tf_op jit(solution)/shard_map/pallas_call | solution.py:154
  67.8 2.9 %shard_map.57.refs_3_ = bf16[16,144,1024]{2,1,0:T(8,128)(2,1)S(1)} custom-call(bf16[144,2240]{1,0:T(8,128)(2,1)S(1)} %collective-permute-done.3.refs_0_, bf16[144,2240]{1,0:T(8,128)(2,1)S(1)} %collective-permute-done.4.refs_1_, bf16[144,2240]{1,0:T(8,128)(2,1)S(1)} %collective-permute-done.17.refs_2_, ...), custom_call_target="tpu_custom_call", output_to_operand_aliasing={{}: (5, {})} | custom-call | flops 2642411520 | bytes 3760128 | tf_op jit(solution)/shard_map/pallas_call | solution.py:154
  70.7 2.6 %collective-permute-done.15.refs_0_ = bf16[144,2240]{1,0:T(8,128)(2,1)S(1)} collective-permute-done((bf16[144,2240]{1,0:T(8,128)(2,1)S(1)}, bf16[144,2240]{1,0:T(8,128)(2,1)S(1)}, u32[]{:S(2)}, u32[]{:S(2)}) %collective-permute-start.15) | collective-permute-done | bytes 645152 | tf_op jit(solution)/shard_map/ppermute | solution.py:88
  73.4 5.1 %collective-permute-start.21 = (bf16[144,2240]{1,0:T(8,128)(2,1)S(1)}, bf16[144,2240]{1,0:T(8,128)(2,1)S(1)}, u32[]{:S(2)}, u32[]{:S(2)}) collective-permute-start(bf16[144,2240]{1,0:T(8,128)(2,1)S(1)} %collective-permute-done.15.refs_0_), channel_id=1, source_target_pairs={{0,1},{1,0},{2,3},{3,2},{4,5},{5,4},{6,7},{7,6},{8,9},{9,8},{10,11... | collective-permute-start | bytes 1935368 | tf_op jit(solution)/shard_map/ppermute | solution.py:88
  78.7 1.2 collective-permute-start.14
  80.0 1.6 shard_map.59.refs_3_
  81.5 1.6 shard_map.60
  83.1 1.9 %shard_map.61 = f32[320,128]{1,0:T(8,128)S(1)} custom-call(s32[3]{0:T(128)S(1)} %pad_add_fusion.at_ref, bf16[32,72,1024]{2,1,0:T(8,128)(2,1)S(1)} %bitcast.16), custom_call_target="tpu_custom_call" | custom-call | flops 301989888 | bytes 4718592 | tf_op jit(solution)/shard_map/pallas_call | solution.py:214
  85.1 1.1 collective-permute-start.23
  86.7 1.0 collective-permute-start.27
  87.7 0.6 collective-permute-done.13.refs_0_.refs_3_
  88.3 1.5 collective-permute-done.14.refs_1_.refs_6_
  89.8 2.3 %collective-permute-start.30 = (bf16[144,2240]{1,0:T(8,128)(2,1)S(1)}, bf16[144,2240]{1,0:T(8,128)(2,1)S(1)}, u32[]{:S(2)}, u32[]{:S(2)}) collective-permute-start(bf16[144,2240]{1,0:T(8,128)(2,1)S(1)} %collective-permute-done.13.refs_0_.refs_3_), channel_id=1, source_target_pairs={{0,1},{1,0},{2,3},{3,2},{4,5},{5,4},{6,7},{7,6},{8,9},{9,8},{10,11... | collective-permute-start | bytes 1935368 | tf_op jit(solution)/shard_map/ppermute | solution.py:88
  92.1 1.3 collective-permute-start.28
  93.7 1.5 collective-permute-done.28
  95.3 0.8 collective-permute-done.26.refs_2_
  96.0 1.7 collective-permute-done.27.refs_3_.refs_7_
  97.7 2.9 %collective-permute-start.32 = (bf16[144,2240]{1,0:T(8,128)(2,1)S(1)}, bf16[144,2240]{1,0:T(8,128)(2,1)S(1)}, u32[]{:S(2)}, u32[]{:S(2)}) collective-permute-start(bf16[144,2240]{1,0:T(8,128)(2,1)S(1)} %collective-permute-done.26.refs_2_), channel_id=1, source_target_pairs={{0,1},{1,0},{2,3},{3,2},{4,5},{5,4},{6,7},{7,6},{8,9},{9,8},{10,11... | collective-permute-start | bytes 1935368 | tf_op jit(solution)/shard_map/ppermute | solution.py:88
  100.6 2.9 %collective-permute-start.29 = (f32[1,40,128]{2,1,0:T(8,128)S(1)}, f32[1,40,128]{2,1,0:T(8,128)S(1)}, u32[]{:S(2)}, u32[]{:S(2)}) collective-permute-start(f32[1,40,128]{2,1,0:T(8,128)S(1)} %constant_dynamic-slice_fusion), channel_id=1, source_target_pairs={{0,4},{1,5},{2,6},{3,7},{4,0},{5,1},{6,2},{7,3},{8,12},{9,13},{10,... | collective-permute-start | bytes 61448 | tf_op jit(solution)/shard_map/ppermute | solution.py:317
  103.5 1.2 collective-permute-done.29
  104.8 2.7 %collective-permute-start.25 = (bf16[144,2240]{1,0:T(8,128)(2,1)S(1)}, bf16[144,2240]{1,0:T(8,128)(2,1)S(1)}, u32[]{:S(2)}, u32[]{:S(2)}) collective-permute-start(bf16[144,2240]{1,0:T(8,128)(2,1)S(1)} %collective-permute-done.13.refs_0_.refs_3_), channel_id=1, source_target_pairs={{0,96},{1,25},{2,98},{3,27},{4,100},{5,29},{6,102},{7,31},{8,104},... | collective-permute-start | bytes 1935368 | tf_op jit(solution)/shard_map/ppermute | solution.py:88
  107.5 4.4 %shard_map.62.refs_5_ = bf16[8,144,1024]{2,1,0:T(8,128)(2,1)S(1)} custom-call(s32[3]{0:T(128)S(1)} %pad_add_fusion.at_ref, bf16[144,2240]{1,0:T(8,128)(2,1)S(1)} %collective-permute-done.13.refs_0_.refs_3_, bf16[144,2240]{1,0:T(8,128)(2,1)S(1)} %collective-permute-done.14.refs_1_.refs_6_, ...), custom_call_target="tpu_custom_call", output_to_operand_aliasing={{}: (10, {})} | custom-call | flops 2642411520 | bytes 3760128 | tf_op jit(solution)/shard_map/pallas_call | solution.py:154
  111.9 3.9 %collective-permute-done.24.refs_0_.refs_4_ = bf16[144,2240]{1,0:T(8,128)(2,1)S(1)} collective-permute-done((bf16[144,2240]{1,0:T(8,128)(2,1)S(1)}, bf16[144,2240]{1,0:T(8,128)(2,1)S(1)}, u32[]{:S(2)}, u32[]{:S(2)}) %collective-permute-start.24) | collective-permute-done | bytes 645152 | tf_op jit(solution)/shard_map/ppermute | solution.py:88
  115.8 2.5 %collective-permute-start.38 = (bf16[144,2240]{1,0:T(8,128)(2,1)S(1)}, bf16[144,2240]{1,0:T(8,128)(2,1)S(1)}, u32[]{:S(2)}, u32[]{:S(2)}) collective-permute-start(bf16[144,2240]{1,0:T(8,128)(2,1)S(1)} %collective-permute-done.24.refs_0_.refs_4_), channel_id=1, source_target_pairs={{0,1},{1,0},{2,3},{3,2},{4,5},{5,4},{6,7},{7,6},{8,9},{9,8},{10,11... | collective-permute-start | bytes 1935368 | tf_op jit(solution)/shard_map/ppermute | solution.py:88
  118.3 1.3 collective-permute-start.34
  119.6 0.9 collective-permute-done.34
  120.5 4.2 %collective-permute-start.35 = (f32[1,40,128]{2,1,0:T(8,128)S(1)}, f32[1,40,128]{2,1,0:T(8,128)S(1)}, u32[]{:S(2)}, u32[]{:S(2)}) collective-permute-start(f32[1,40,128]{2,1,0:T(8,128)S(1)} %add.50), channel_id=1, source_target_pairs={{0,16},{8,24},{16,32},{24,40},{32,48},{40,56},{48,64},{56,72},{64,... | collective-permute-start | bytes 61448 | tf_op jit(solution)/shard_map/ppermute | solution.py:330
  124.7 0.9 collective-permute-done.35
  125.6 7.2 %collective-permute-start.36 = (f32[1,40,128]{2,1,0:T(8,128)S(1)}, f32[1,40,128]{2,1,0:T(8,128)S(1)}, u32[]{:S(2)}, u32[]{:S(2)}) collective-permute-start(f32[1,40,128]{2,1,0:T(8,128)S(1)} %add.51), channel_id=1, source_target_pairs={{0,32},{8,40},{16,48},{24,56},{32,64},{40,72},{48,80},{56,88},{64,... | collective-permute-start | bytes 61448 | tf_op jit(solution)/shard_map/ppermute | solution.py:330
  132.8 0.9 collective-permute-done.36
  133.7 7.0 %collective-permute-start.37 = (f32[1,40,128]{2,1,0:T(8,128)S(1)}, f32[1,40,128]{2,1,0:T(8,128)S(1)}, u32[]{:S(2)}, u32[]{:S(2)}) collective-permute-start(f32[1,40,128]{2,1,0:T(8,128)S(1)} %add.52), channel_id=1, source_target_pairs={{0,64},{8,72},{16,80},{24,88},{32,96},{40,104},{48,112},{56,120},{... | collective-permute-start | bytes 61448 | tf_op jit(solution)/shard_map/ppermute | solution.py:330
  140.7 0.9 collective-permute-done.37
  141.6 2.6 %shard_map.63 = bf16[8,144,1024]{2,1,0:T(8,128)(2,1)S(1)} custom-call(s32[3]{0:T(128)S(1)} %pad_add_fusion.at_ref, bf16[144,2240]{1,0:T(8,128)(2,1)S(1)} %collective-permute-done.24.refs_0_.refs_4_, bf16[144,2240]{1,0:T(8,128)(2,1)S(1)} %collective-permute-done.25.refs_1_.refs_5_, ...), custom_call_target="tpu_custom_call", output_to_operand_aliasing={{}: (6, {})} | custom-call | flops 1321205760 | bytes 1880064 | tf_op jit(solution)/shard_map/pallas_call | solution.py:154
  144.2 3.0 %collective-permute-start.40 = (f32[1,40,128]{2,1,0:T(8,128)S(1)}, f32[1,40,128]{2,1,0:T(8,128)S(1)}, u32[]{:S(2)}, u32[]{:S(2)}) collective-permute-start(f32[1,40,128]{2,1,0:T(8,128)S(1)} %add.53), channel_id=1, source_target_pairs={{0,4},{1,5},{2,6},{3,7},{4,0},{5,1},{6,2},{7,3},{8,12},{9,13},{10,... | collective-permute-start | bytes 61448 | tf_op jit(solution)/shard_map/ppermute | solution.py:317
  147.2 1.2 collective-permute-done.40
  148.4 1.3 collective-permute-start.41
  149.7 1.6 collective-permute-done.41
  151.3 7.0 %collective-permute-start.42 = (f32[4,40,128]{2,1,0:T(8,128)S(1)}, f32[4,40,128]{2,1,0:T(8,128)S(1)}, u32[]{:S(2)}, u32[]{:S(2)}) collective-permute-start(f32[4,40,128]{2,1,0:T(8,128)S(1)} %maximum_select_fusion.1), channel_id=1, source_target_pairs={{0,1},{1,0},{2,3},{3,2},{4,5},{5,4},{6,7},{7,6},{8,9},{9,8},{10,11... | collective-permute-start | bytes 245768 | tf_op jit(solution)/shard_map/ppermute | solution.py:317
  158.3 0.9 collective-permute-done.42
  159.2 12.9 %shard_map.64 = bf16[2240,1024]{1,0:T(8,128)(2,1)} custom-call(s32[3]{0:T(128)S(1)} %pad_add_fusion.at_ref, bf16[16,72,1024]{2,1,0:T(8,128)(2,1)S(1)} %bitcast.17, f32[320,128]{1,0:T(8,128)S(1)} %bitcast.20, bf16[144,2240]{1,0:T(8,128)(2,1)S(1)} %pad_maximum_fusion.3.refs_0_, bf16[144,2240]{1,0:T(8,128)(2,1)S(1)} %pad_maximum_fusion.4.refs_1_, ...), custom_call_target="tpu_custom_call" | custom-call | flops 6492782592 | bytes 14336000 | tf_op jit(solution)/shard_map/pallas_call | solution.py:290
  (69 shorter events, 2.0 us)
Async XLA Ops:
  0.0 10.4 %copy-start.4 = (f32[2240]{0:T(1024)S(1)}, f32[2240]{0:T(1024)}, u32[]{:S(2)}) copy-start(f32[2240]{0:T(1024)} %param.6) | copy-start | bytes 26884
  0.0 10.4 %copy-start.1 = (bf16[1024,2240]{0,1:T(8,128)(2,1)S(1)}, bf16[1024,2240]{0,1:T(8,128)(2,1)}, u32[]{:S(2)}) copy-start(bf16[1024,2240]{0,1:T(8,128)(2,1)} %param.5) | copy-start | bytes 13762564
  1.2 12.2 %collective-permute-start = (bf16[72,2240]{1,0:T(8,128)(2,1)S(1)}, bf16[72,2240]{1,0:T(8,128)(2,1)S(1)}, u32[]{:S(2)}, u32[]{:S(2)}) collective-permute-start(bf16[72,2240]{1,0:T(8,128)(2,1)S(1)} %dynamic-slice_bitcast_fusion), channel_id=1, source_target_pairs={{0,80},{80,0},{1,96},{97,1},{8,72},{72,8},{9,104},{105,9},{16,48},... | collective-permute-start | bytes 967688 | tf_op jit(solution)/shard_map/ppermute | solution.py:352
  10.4 3.0 %copy-start.2 = (bf16[2240,216]{0,1:T(8,128)(2,1)S(1)}, bf16[2240,216]{0,1:T(8,128)(2,1)}, u32[]{:S(2)}) copy-start(bf16[2240,216]{0,1:T(8,128)(2,1)} %param.7) | copy-start | bytes 2903044
  10.4 3.0 %copy-start.3 = (bf16[72,2240]{1,0:T(8,128)(2,1)S(1)}, bf16[72,2240]{1,0:T(8,128)(2,1)}, u32[]{:S(2)}) copy-start(bf16[72,2240]{1,0:T(8,128)(2,1)} %param.8) | copy-start | bytes 967684
  13.4 30.5 %copy-start = (bf16[2240,1024]{1,0:T(8,128)(2,1)S(1)}, bf16[2240,1024]{1,0:T(8,128)(2,1)}, u32[]{:S(2)}) copy-start(bf16[2240,1024]{1,0:T(8,128)(2,1)} %fusion.3.refs_4_.refs_2_.refs_8_) | copy-start | bytes 13762564
  13.7 15.3 %collective-permute-start.5 = (bf16[144,2240]{1,0:T(8,128)(2,1)S(1)}, bf16[144,2240]{1,0:T(8,128)(2,1)S(1)}, u32[]{:S(2)}, u32[]{:S(2)}) collective-permute-start(bf16[144,2240]{1,0:T(8,128)(2,1)S(1)} %pad_maximum_fusion), channel_id=1, source_target_pairs={{0,24},{1,97},{2,26},{3,99},{4,28},{5,101},{6,30},{7,103},{8,0},{9... | collective-permute-start | bytes 1935368 | tf_op jit(solution)/shard_map/ppermute | solution.py:88
  13.8 13.0 %collective-permute-start.1 = (bf16[144,2240]{1,0:T(8,128)(2,1)S(1)}, bf16[144,2240]{1,0:T(8,128)(2,1)S(1)}, u32[]{:S(2)}, u32[]{:S(2)}) collective-permute-start(bf16[144,2240]{1,0:T(8,128)(2,1)S(1)} %pad_maximum_fusion), channel_id=1, source_target_pairs={{0,8},{1,33},{2,10},{3,35},{4,12},{5,37},{6,14},{7,39},{8,16},{9,4... | collective-permute-start | bytes 1935368 | tf_op jit(solution)/shard_map/ppermute | solution.py:88
  26.8 7.6 %collective-permute-start.2 = (bf16[72,2240]{1,0:T(8,128)(2,1)S(1)}, bf16[72,2240]{1,0:T(8,128)(2,1)S(1)}, u32[]{:S(2)}, u32[]{:S(2)}) collective-permute-start(bf16[72,2240]{1,0:T(8,128)(2,1)S(1)} %get-tuple-element.78), channel_id=1, source_target_pairs={{0,8},{1,33},{2,10},{3,35},{4,12},{5,37},{6,14},{7,39},{8,16},{9,4... | collective-permute-start | bytes 967688 | tf_op jit(solution)/shard_map/ppermute | solution.py:88
  29.1 13.3 %collective-permute-start.8 = (bf16[144,2240]{1,0:T(8,128)(2,1)S(1)}, bf16[144,2240]{1,0:T(8,128)(2,1)S(1)}, u32[]{:S(2)}, u32[]{:S(2)}) collective-permute-start(bf16[144,2240]{1,0:T(8,128)(2,1)S(1)} %pad_maximum_fusion.2.refs_0_), channel_id=1, source_target_pairs={{0,1},{1,0},{2,3},{3,2},{4,5},{5,4},{6,7},{7,6},{8,9},{9,8},{10,11... | collective-permute-start | bytes 1935368 | tf_op jit(solution)/shard_map/ppermute | solution.py:88
  34.5 7.9 %collective-permute-start.9 = (bf16[144,2240]{1,0:T(8,128)(2,1)S(1)}, bf16[144,2240]{1,0:T(8,128)(2,1)S(1)}, u32[]{:S(2)}, u32[]{:S(2)}) collective-permute-start(bf16[144,2240]{1,0:T(8,128)(2,1)S(1)} %pad_maximum_fusion.1.refs_1_), channel_id=1, source_target_pairs={{0,1},{1,0},{2,3},{3,2},{4,5},{5,4},{6,7},{7,6},{8,9},{9,8},{10,11... | collective-permute-start | bytes 1935368 | tf_op jit(solution)/shard_map/ppermute | solution.py:88
  38.3 11.0 %collective-permute-start.6 = (bf16[144,2240]{1,0:T(8,128)(2,1)S(1)}, bf16[144,2240]{1,0:T(8,128)(2,1)S(1)}, u32[]{:S(2)}, u32[]{:S(2)}) collective-permute-start(bf16[144,2240]{1,0:T(8,128)(2,1)S(1)} %pad_maximum_fusion.2.refs_0_), channel_id=1, source_target_pairs={{0,32},{1,9},{2,34},{3,11},{4,36},{5,13},{6,38},{7,15},{8,40},{9,1... | collective-permute-start | bytes 1935368 | tf_op jit(solution)/shard_map/ppermute | solution.py:88
  38.3 13.8 %collective-permute-start.7 = (bf16[144,2240]{1,0:T(8,128)(2,1)S(1)}, bf16[144,2240]{1,0:T(8,128)(2,1)S(1)}, u32[]{:S(2)}, u32[]{:S(2)}) collective-permute-start(bf16[144,2240]{1,0:T(8,128)(2,1)S(1)} %pad_maximum_fusion.2.refs_0_), channel_id=1, source_target_pairs={{0,96},{1,25},{2,98},{3,27},{4,100},{5,29},{6,102},{7,31},{8,104},... | collective-permute-start | bytes 1935368 | tf_op jit(solution)/shard_map/ppermute | solution.py:88
  40.9 13.8 %collective-permute-start.12 = (bf16[72,2240]{1,0:T(8,128)(2,1)S(1)}, bf16[72,2240]{1,0:T(8,128)(2,1)S(1)}, u32[]{:S(2)}, u32[]{:S(2)}) collective-permute-start(bf16[72,2240]{1,0:T(8,128)(2,1)S(1)} %get-tuple-element.81), channel_id=1, source_target_pairs={{0,24},{1,97},{2,26},{3,99},{4,28},{5,101},{6,30},{7,103},{8,0},{9... | collective-permute-start | bytes 967688 | tf_op jit(solution)/shard_map/ppermute | solution.py:88
  42.4 17.9 %collective-permute-start.3 = (bf16[144,2240]{1,0:T(8,128)(2,1)S(1)}, bf16[144,2240]{1,0:T(8,128)(2,1)S(1)}, u32[]{:S(2)}, u32[]{:S(2)}) collective-permute-start(bf16[144,2240]{1,0:T(8,128)(2,1)S(1)} %pad_maximum_fusion.1.refs_1_), channel_id=1, source_target_pairs={{0,96},{1,25},{2,98},{3,27},{4,100},{5,29},{6,102},{7,31},{8,104},... | collective-permute-start | bytes 1935368 | tf_op jit(solution)/shard_map/ppermute | solution.py:88
  42.4 17.9 %collective-permute-start.4 = (bf16[144,2240]{1,0:T(8,128)(2,1)S(1)}, bf16[144,2240]{1,0:T(8,128)(2,1)S(1)}, u32[]{:S(2)}, u32[]{:S(2)}) collective-permute-start(bf16[144,2240]{1,0:T(8,128)(2,1)S(1)} %pad_maximum_fusion.1.refs_1_), channel_id=1, source_target_pairs={{0,32},{1,9},{2,34},{3,11},{4,36},{5,13},{6,38},{7,15},{8,40},{9,1... | collective-permute-start | bytes 1935368 | tf_op jit(solution)/shard_map/ppermute | solution.py:88
  52.1 4.3 %collective-permute-start.10 = (bf16[144,2240]{1,0:T(8,128)(2,1)S(1)}, bf16[144,2240]{1,0:T(8,128)(2,1)S(1)}, u32[]{:S(2)}, u32[]{:S(2)}) collective-permute-start(bf16[144,2240]{1,0:T(8,128)(2,1)S(1)} %collective-permute-done.7.refs_0_), channel_id=1, source_target_pairs={{0,1},{1,0},{2,3},{3,2},{4,5},{5,4},{6,7},{7,6},{8,9},{9,8},{10,11... | collective-permute-start | bytes 1935368 | tf_op jit(solution)/shard_map/ppermute | solution.py:88
  54.7 2.7 %collective-permute-start.11 = (bf16[144,2240]{1,0:T(8,128)(2,1)S(1)}, bf16[144,2240]{1,0:T(8,128)(2,1)S(1)}, u32[]{:S(2)}, u32[]{:S(2)}) collective-permute-start(bf16[144,2240]{1,0:T(8,128)(2,1)S(1)} %collective-permute-done.6.refs_1_), channel_id=1, source_target_pairs={{0,1},{1,0},{2,3},{3,2},{4,5},{5,4},{6,7},{7,6},{8,9},{9,8},{10,11... | collective-permute-start | bytes 1935368 | tf_op jit(solution)/shard_map/ppermute | solution.py:88
  60.3 3.2 %collective-permute-start.19 = (bf16[144,2240]{1,0:T(8,128)(2,1)S(1)}, bf16[144,2240]{1,0:T(8,128)(2,1)S(1)}, u32[]{:S(2)}, u32[]{:S(2)}) collective-permute-start(bf16[144,2240]{1,0:T(8,128)(2,1)S(1)} %pad_maximum_fusion.3.refs_0_), channel_id=1, source_target_pairs={{0,1},{1,0},{2,3},{3,2},{4,5},{5,4},{6,7},{7,6},{8,9},{9,8},{10,11... | collective-permute-start | bytes 1935368 | tf_op jit(solution)/shard_map/ppermute | solution.py:88
  61.8 3.2 %collective-permute-start.20 = (bf16[144,2240]{1,0:T(8,128)(2,1)S(1)}, bf16[144,2240]{1,0:T(8,128)(2,1)S(1)}, u32[]{:S(2)}, u32[]{:S(2)}) collective-permute-start(bf16[144,2240]{1,0:T(8,128)(2,1)S(1)} %pad_maximum_fusion.4.refs_1_), channel_id=1, source_target_pairs={{0,1},{1,0},{2,3},{3,2},{4,5},{5,4},{6,7},{7,6},{8,9},{9,8},{10,11... | collective-permute-start | bytes 1935368 | tf_op jit(solution)/shard_map/ppermute | solution.py:88
  61.8 6.0 %collective-permute-start.17 = (bf16[144,2240]{1,0:T(8,128)(2,1)S(1)}, bf16[144,2240]{1,0:T(8,128)(2,1)S(1)}, u32[]{:S(2)}, u32[]{:S(2)}) collective-permute-start(bf16[144,2240]{1,0:T(8,128)(2,1)S(1)} %collective-permute-done.3.refs_0_), channel_id=1, source_target_pairs={{0,1},{1,0},{2,3},{3,2},{4,5},{5,4},{6,7},{7,6},{8,9},{9,8},{10,11... | collective-permute-start | bytes 1935368 | tf_op jit(solution)/shard_map/ppermute | solution.py:88
  62.3 5.5 %collective-permute-start.18 = (bf16[144,2240]{1,0:T(8,128)(2,1)S(1)}, bf16[144,2240]{1,0:T(8,128)(2,1)S(1)}, u32[]{:S(2)}, u32[]{:S(2)}) collective-permute-start(bf16[144,2240]{1,0:T(8,128)(2,1)S(1)} %collective-permute-done.4.refs_1_), channel_id=1, source_target_pairs={{0,1},{1,0},{2,3},{3,2},{4,5},{5,4},{6,7},{7,6},{8,9},{9,8},{10,11... | collective-permute-start | bytes 1935368 | tf_op jit(solution)/shard_map/ppermute | solution.py:88
  62.3 11.0 %collective-permute-start.15 = (bf16[144,2240]{1,0:T(8,128)(2,1)S(1)}, bf16[144,2240]{1,0:T(8,128)(2,1)S(1)}, u32[]{:S(2)}, u32[]{:S(2)}) collective-permute-start(bf16[144,2240]{1,0:T(8,128)(2,1)S(1)} %collective-permute-done.6.refs_1_), channel_id=1, source_target_pairs={{0,32},{1,9},{2,34},{3,11},{4,36},{5,13},{6,38},{7,15},{8,40},{9,1... | collective-permute-start | bytes 1935368 | tf_op jit(solution)/shard_map/ppermute | solution.py:88
  63.5 9.8 %collective-permute-start.16 = (bf16[144,2240]{1,0:T(8,128)(2,1)S(1)}, bf16[144,2240]{1,0:T(8,128)(2,1)S(1)}, u32[]{:S(2)}, u32[]{:S(2)}) collective-permute-start(bf16[144,2240]{1,0:T(8,128)(2,1)S(1)} %collective-permute-done.3.refs_0_), channel_id=1, source_target_pairs={{0,96},{1,25},{2,98},{3,27},{4,100},{5,29},{6,102},{7,31},{8,104},... | collective-permute-start | bytes 1935368 | tf_op jit(solution)/shard_map/ppermute | solution.py:88
  73.4 8.2 %collective-permute-start.21 = (bf16[144,2240]{1,0:T(8,128)(2,1)S(1)}, bf16[144,2240]{1,0:T(8,128)(2,1)S(1)}, u32[]{:S(2)}, u32[]{:S(2)}) collective-permute-start(bf16[144,2240]{1,0:T(8,128)(2,1)S(1)} %collective-permute-done.15.refs_0_), channel_id=1, source_target_pairs={{0,1},{1,0},{2,3},{3,2},{4,5},{5,4},{6,7},{7,6},{8,9},{9,8},{10,11... | collective-permute-start | bytes 1935368 | tf_op jit(solution)/shard_map/ppermute | solution.py:88
  78.5 3.1 %collective-permute-start.22 = (bf16[144,2240]{1,0:T(8,128)(2,1)S(1)}, bf16[144,2240]{1,0:T(8,128)(2,1)S(1)}, u32[]{:S(2)}, u32[]{:S(2)}) collective-permute-start(bf16[144,2240]{1,0:T(8,128)(2,1)S(1)} %collective-permute-done.16.refs_1_), channel_id=1, source_target_pairs={{0,1},{1,0},{2,3},{3,2},{4,5},{5,4},{6,7},{7,6},{8,9},{9,8},{10,11... | collective-permute-start | bytes 1935368 | tf_op jit(solution)/shard_map/ppermute | solution.py:88
  78.5 9.8 %collective-permute-start.13 = (bf16[144,2240]{1,0:T(8,128)(2,1)S(1)}, bf16[144,2240]{1,0:T(8,128)(2,1)S(1)}, u32[]{:S(2)}, u32[]{:S(2)}) collective-permute-start(bf16[144,2240]{1,0:T(8,128)(2,1)S(1)} %pad_maximum_fusion.4.refs_1_), channel_id=1, source_target_pairs={{0,96},{1,25},{2,98},{3,27},{4,100},{5,29},{6,102},{7,31},{8,104},... | collective-permute-start | bytes 1935368 | tf_op jit(solution)/shard_map/ppermute | solution.py:88
  78.7 11.0 %collective-permute-start.14 = (bf16[144,2240]{1,0:T(8,128)(2,1)S(1)}, bf16[144,2240]{1,0:T(8,128)(2,1)S(1)}, u32[]{:S(2)}, u32[]{:S(2)}) collective-permute-start(bf16[144,2240]{1,0:T(8,128)(2,1)S(1)} %pad_maximum_fusion.3.refs_0_), channel_id=1, source_target_pairs={{0,32},{1,9},{2,34},{3,11},{4,36},{5,13},{6,38},{7,15},{8,40},{9,1... | collective-permute-start | bytes 1935368 | tf_op jit(solution)/shard_map/ppermute | solution.py:88
  85.1 2.6 %collective-permute-start.23 = (f32[4,40,128]{2,1,0:T(8,128)S(1)}, f32[4,40,128]{2,1,0:T(8,128)S(1)}, u32[]{:S(2)}, u32[]{:S(2)}) collective-permute-start(f32[4,40,128]{2,1,0:T(8,128)S(1)} %constant_dynamic-slice_fusion.2), channel_id=1, source_target_pairs={{0,1},{1,0},{2,3},{3,2},{4,5},{5,4},{6,7},{7,6},{8,9},{9,8},{10,11... | collective-permute-start | bytes 245768 | tf_op jit(solution)/shard_map/ppermute | solution.py:317
  86.2 9.8 %collective-permute-start.26 = (bf16[144,2240]{1,0:T(8,128)(2,1)S(1)}, bf16[144,2240]{1,0:T(8,128)(2,1)S(1)}, u32[]{:S(2)}, u32[]{:S(2)}) collective-permute-start(bf16[144,2240]{1,0:T(8,128)(2,1)S(1)} %pad_maximum_fusion.3.refs_0_), channel_id=1, source_target_pairs={{0,96},{1,25},{2,98},{3,27},{4,100},{5,29},{6,102},{7,31},{8,104},... | collective-permute-start | bytes 1935368 | tf_op jit(solution)/shard_map/ppermute | solution.py:88
  86.7 11.0 %collective-permute-start.27 = (bf16[144,2240]{1,0:T(8,128)(2,1)S(1)}, bf16[144,2240]{1,0:T(8,128)(2,1)S(1)}, u32[]{:S(2)}, u32[]{:S(2)}) collective-permute-start(bf16[144,2240]{1,0:T(8,128)(2,1)S(1)} %pad_maximum_fusion.4.refs_1_), channel_id=1, source_target_pairs={{0,32},{1,9},{2,34},{3,11},{4,36},{5,13},{6,38},{7,15},{8,40},{9,1... | collective-permute-start | bytes 1935368 | tf_op jit(solution)/shard_map/ppermute | solution.py:88
  89.8 15.0 %collective-permute-start.30 = (bf16[144,2240]{1,0:T(8,128)(2,1)S(1)}, bf16[144,2240]{1,0:T(8,128)(2,1)S(1)}, u32[]{:S(2)}, u32[]{:S(2)}) collective-permute-start(bf16[144,2240]{1,0:T(8,128)(2,1)S(1)} %collective-permute-done.13.refs_0_.refs_3_), channel_id=1, source_target_pairs={{0,1},{1,0},{2,3},{3,2},{4,5},{5,4},{6,7},{7,6},{8,9},{9,8},{10,11... | collective-permute-start | bytes 1935368 | tf_op jit(solution)/shard_map/ppermute | solution.py:88
  92.1 3.2 %collective-permute-start.28 = (f32[2,40,128]{2,1,0:T(8,128)S(1)}, f32[2,40,128]{2,1,0:T(8,128)S(1)}, u32[]{:S(2)}, u32[]{:S(2)}) collective-permute-start(f32[2,40,128]{2,1,0:T(8,128)S(1)} %constant_dynamic-slice_fusion.1), channel_id=1, source_target_pairs={{0,2},{1,3},{2,0},{3,1},{4,6},{5,7},{6,4},{7,5},{8,10},{9,11},{10,... | collective-permute-start | bytes 122888 | tf_op jit(solution)/shard_map/ppermute | solution.py:317
  93.4 14.0 %collective-permute-start.31 = (bf16[144,2240]{1,0:T(8,128)(2,1)S(1)}, bf16[144,2240]{1,0:T(8,128)(2,1)S(1)}, u32[]{:S(2)}, u32[]{:S(2)}) collective-permute-start(bf16[144,2240]{1,0:T(8,128)(2,1)S(1)} %collective-permute-done.14.refs_1_.refs_6_), channel_id=1, source_target_pairs={{0,1},{1,0},{2,3},{3,2},{4,5},{5,4},{6,7},{7,6},{8,9},{9,8},{10,11... | collective-permute-start | bytes 1935368 | tf_op jit(solution)/shard_map/ppermute | solution.py:88
  97.7 9.7 %collective-permute-start.32 = (bf16[144,2240]{1,0:T(8,128)(2,1)S(1)}, bf16[144,2240]{1,0:T(8,128)(2,1)S(1)}, u32[]{:S(2)}, u32[]{:S(2)}) collective-permute-start(bf16[144,2240]{1,0:T(8,128)(2,1)S(1)} %collective-permute-done.26.refs_2_), channel_id=1, source_target_pairs={{0,1},{1,0},{2,3},{3,2},{4,5},{5,4},{6,7},{7,6},{8,9},{9,8},{10,11... | collective-permute-start | bytes 1935368 | tf_op jit(solution)/shard_map/ppermute | solution.py:88
  100.6 6.8 %collective-permute-start.33 = (bf16[144,2240]{1,0:T(8,128)(2,1)S(1)}, bf16[144,2240]{1,0:T(8,128)(2,1)S(1)}, u32[]{:S(2)}, u32[]{:S(2)}) collective-permute-start(bf16[144,2240]{1,0:T(8,128)(2,1)S(1)} %collective-permute-done.27.refs_3_.refs_7_), channel_id=1, source_target_pairs={{0,1},{1,0},{2,3},{3,2},{4,5},{5,4},{6,7},{7,6},{8,9},{9,8},{10,11... | collective-permute-start | bytes 1935368 | tf_op jit(solution)/shard_map/ppermute | solution.py:88
  100.6 4.1 %collective-permute-start.29 = (f32[1,40,128]{2,1,0:T(8,128)S(1)}, f32[1,40,128]{2,1,0:T(8,128)S(1)}, u32[]{:S(2)}, u32[]{:S(2)}) collective-permute-start(f32[1,40,128]{2,1,0:T(8,128)S(1)} %constant_dynamic-slice_fusion), channel_id=1, source_target_pairs={{0,4},{1,5},{2,6},{3,7},{4,0},{5,1},{6,2},{7,3},{8,12},{9,13},{10,... | collective-permute-start | bytes 61448 | tf_op jit(solution)/shard_map/ppermute | solution.py:317
  104.8 11.0 %collective-permute-start.24 = (bf16[144,2240]{1,0:T(8,128)(2,1)S(1)}, bf16[144,2240]{1,0:T(8,128)(2,1)S(1)}, u32[]{:S(2)}, u32[]{:S(2)}) collective-permute-start(bf16[144,2240]{1,0:T(8,128)(2,1)S(1)} %collective-permute-done.14.refs_1_.refs_6_), channel_id=1, source_target_pairs={{0,32},{1,9},{2,34},{3,11},{4,36},{5,13},{6,38},{7,15},{8,40},{9,1... | collective-permute-start | bytes 1935368 | tf_op jit(solution)/shard_map/ppermute | solution.py:88
  104.8 11.0 %collective-permute-start.25 = (bf16[144,2240]{1,0:T(8,128)(2,1)S(1)}, bf16[144,2240]{1,0:T(8,128)(2,1)S(1)}, u32[]{:S(2)}, u32[]{:S(2)}) collective-permute-start(bf16[144,2240]{1,0:T(8,128)(2,1)S(1)} %collective-permute-done.13.refs_0_.refs_3_), channel_id=1, source_target_pairs={{0,96},{1,25},{2,98},{3,27},{4,100},{5,29},{6,102},{7,31},{8,104},... | collective-permute-start | bytes 1935368 | tf_op jit(solution)/shard_map/ppermute | solution.py:88
  115.8 25.8 %collective-permute-start.38 = (bf16[144,2240]{1,0:T(8,128)(2,1)S(1)}, bf16[144,2240]{1,0:T(8,128)(2,1)S(1)}, u32[]{:S(2)}, u32[]{:S(2)}) collective-permute-start(bf16[144,2240]{1,0:T(8,128)(2,1)S(1)} %collective-permute-done.24.refs_0_.refs_4_), channel_id=1, source_target_pairs={{0,1},{1,0},{2,3},{3,2},{4,5},{5,4},{6,7},{7,6},{8,9},{9,8},{10,11... | collective-permute-start | bytes 1935368 | tf_op jit(solution)/shard_map/ppermute | solution.py:88
  118.3 23.3 %collective-permute-start.39 = (bf16[144,2240]{1,0:T(8,128)(2,1)S(1)}, bf16[144,2240]{1,0:T(8,128)(2,1)S(1)}, u32[]{:S(2)}, u32[]{:S(2)}) collective-permute-start(bf16[144,2240]{1,0:T(8,128)(2,1)S(1)} %collective-permute-done.25.refs_1_.refs_5_), channel_id=1, source_target_pairs={{0,1},{1,0},{2,3},{3,2},{4,5},{5,4},{6,7},{7,6},{8,9},{9,8},{10,11... | collective-permute-start | bytes 1935368 | tf_op jit(solution)/shard_map/ppermute | solution.py:88
  118.3 2.2 %collective-permute-start.34 = (f32[1,40,128]{2,1,0:T(8,128)S(1)}, f32[1,40,128]{2,1,0:T(8,128)S(1)}, u32[]{:S(2)}, u32[]{:S(2)}) collective-permute-start(f32[1,40,128]{2,1,0:T(8,128)S(1)} %dynamic-slice_add_fusion.2), channel_id=1, source_target_pairs={{0,8},{8,16},{16,24},{24,32},{32,40},{40,48},{48,56},{56,64},{64,7... | collective-permute-start | bytes 61448 | tf_op jit(solution)/shard_map/ppermute | solution.py:330
  120.5 5.1 %collective-permute-start.35 = (f32[1,40,128]{2,1,0:T(8,128)S(1)}, f32[1,40,128]{2,1,0:T(8,128)S(1)}, u32[]{:S(2)}, u32[]{:S(2)}) collective-permute-start(f32[1,40,128]{2,1,0:T(8,128)S(1)} %add.50), channel_id=1, source_target_pairs={{0,16},{8,24},{16,32},{24,40},{32,48},{40,56},{48,64},{56,72},{64,... | collective-permute-start | bytes 61448 | tf_op jit(solution)/shard_map/ppermute | solution.py:330
  125.6 8.1 %collective-permute-start.36 = (f32[1,40,128]{2,1,0:T(8,128)S(1)}, f32[1,40,128]{2,1,0:T(8,128)S(1)}, u32[]{:S(2)}, u32[]{:S(2)}) collective-permute-start(f32[1,40,128]{2,1,0:T(8,128)S(1)} %add.51), channel_id=1, source_target_pairs={{0,32},{8,40},{16,48},{24,56},{32,64},{40,72},{48,80},{56,88},{64,... | collective-permute-start | bytes 61448 | tf_op jit(solution)/shard_map/ppermute | solution.py:330
  133.7 7.9 %collective-permute-start.37 = (f32[1,40,128]{2,1,0:T(8,128)S(1)}, f32[1,40,128]{2,1,0:T(8,128)S(1)}, u32[]{:S(2)}, u32[]{:S(2)}) collective-permute-start(f32[1,40,128]{2,1,0:T(8,128)S(1)} %add.52), channel_id=1, source_target_pairs={{0,64},{8,72},{16,80},{24,88},{32,96},{40,104},{48,112},{56,120},{... | collective-permute-start | bytes 61448 | tf_op jit(solution)/shard_map/ppermute | solution.py:330
  144.2 4.2 %collective-permute-start.40 = (f32[1,40,128]{2,1,0:T(8,128)S(1)}, f32[1,40,128]{2,1,0:T(8,128)S(1)}, u32[]{:S(2)}, u32[]{:S(2)}) collective-permute-start(f32[1,40,128]{2,1,0:T(8,128)S(1)} %add.53), channel_id=1, source_target_pairs={{0,4},{1,5},{2,6},{3,7},{4,0},{5,1},{6,2},{7,3},{8,12},{9,13},{10,... | collective-permute-start | bytes 61448 | tf_op jit(solution)/shard_map/ppermute | solution.py:317
  148.4 2.9 %collective-permute-start.41 = (f32[2,40,128]{2,1,0:T(8,128)S(1)}, f32[2,40,128]{2,1,0:T(8,128)S(1)}, u32[]{:S(2)}, u32[]{:S(2)}) collective-permute-start(f32[2,40,128]{2,1,0:T(8,128)S(1)} %maximum_select_fusion.2), channel_id=1, source_target_pairs={{0,2},{1,3},{2,0},{3,1},{4,6},{5,7},{6,4},{7,5},{8,10},{9,11},{10,... | collective-permute-start | bytes 122888 | tf_op jit(solution)/shard_map/ppermute | solution.py:317
  151.3 7.9 %collective-permute-start.42 = (f32[4,40,128]{2,1,0:T(8,128)S(1)}, f32[4,40,128]{2,1,0:T(8,128)S(1)}, u32[]{:S(2)}, u32[]{:S(2)}) collective-permute-start(f32[4,40,128]{2,1,0:T(8,128)S(1)} %maximum_select_fusion.1), channel_id=1, source_target_pairs={{0,1},{1,0},{2,3},{3,2},{4,5},{5,4},{6,7},{7,6},{8,9},{9,8},{10,11... | collective-permute-start | bytes 245768 | tf_op jit(solution)/shard_map/ppermute | solution.py:317
